TPU v7x, 32 devices: a whole 2x2x4 slice. The times are simulated.
32 devices in a mesh: frame: 4 (over x, core), tile: 8 (over z, y).
Axes of the slice: x: 2, y: 2, z: 4, core: 2. Of those that a mesh axis runs over, the one named last changes fastest.
Arguments:
- state_tokens: bfloat16 [16, 8192, 256], P('frame', 'tile'), may hold values from -12 to 12
- gain_time: float32 [256], replicated, may hold values from 0.25 to 1.75
- query_time: bfloat16 [256, 256], replicated, may hold values from -2 to 2
- key_time: bfloat16 [256, 256], replicated, may hold values from -2 to 2
- value_time: bfloat16 [256, 256], replicated, may hold values from -0.375 to 0.375
- output_time: bfloat16 [256, 256], replicated, may hold values from -0.375 to 0.375
- gain_space: float32 [256], replicated, may hold values from 0.25 to 1.75
- query_space: bfloat16 [256, 256], replicated, may hold values from -2 to 2
- key_space: bfloat16 [256, 256], replicated, may hold values from -2 to 2
- value_space: bfloat16 [256, 256], replicated, may hold values from -0.375 to 0.375
- output_space: bfloat16 [256, 256], replicated, may hold values from -0.375 to 0.375
- neighbours: int32 [64, 9], P('tile'), may hold values from -1 to 63, as said below
Outputs:
- updated: bfloat16 [16, 8192, 256], P('frame', 'tile')
Inputs may be any that keep to these rules, and one draw needn't show every extreme that they name: `neighbours`: entry 0 of row b is b itself; the other entries are distinct block ids at most 8 blocks away from b in the cyclic order of the 64 blocks, or -1; only the last entry is ever -1.
All inputs are finite; a program needn't handle non-finite values.
Results may differ from a plain program's by a relative error of at most 0.013.
Values may be sent and summed in bfloat16 or wider, within the bound.
No kernel may reach another device: no remote copies, remote signals or barrier semaphores. Data moves between devices by JAX's collectives and lax.ppermute only.
A program may use at most 128 MiB of HBM per device.

v0:
```python
import jax
import jax.numpy as jnp
from jax import lax
from jax.sharding import PartitionSpec as P

HEADS = 8
BLOCK = 128
NEIGHBOUR_COUNT = 9


EPS = 1e-05
ROT_PERIOD = 1024


def padded(value, sides, width):
    for axis, dim in sides:
        count, length = (lax.axis_size(axis), value.shape[dim])
        up = [(i, (i + 1) % count) for i in range(count)]
        down = [(j, i) for i, j in up]
        last = lax.slice_in_dim(value, length - width, length, axis=dim)
        initial = lax.slice_in_dim(value, 0, width, axis=dim)
        before = lax.ppermute(last, axis, up)
        after = lax.ppermute(initial, axis, down)
        value = jnp.concatenate([before, value, after], axis=dim)
    return value


def rms_scale(rows, gain):
    values = rows.astype(jnp.float32)
    square_mean = jnp.mean(values * values, axis=-1, keepdims=True)
    return (values * lax.rsqrt(square_mean + EPS) * gain).astype(jnp.bfloat16)


def project_rows(rows, weight):
    flat = rows.reshape(-1, rows.shape[-1])
    result = jnp.dot(flat, weight, preferred_element_type=jnp.float32)
    return result.reshape(rows.shape[:-1] + (weight.shape[1],))


def rotate_pairs(values, positions, heads):
    features = values.shape[-1]
    head_dim = features // heads
    half = head_dim // 2
    freqs = jnp.power(10000.0, -jnp.arange(half, dtype=jnp.float32) / half)
    angle = (positions % ROT_PERIOD).astype(jnp.float32)[:, None] * freqs[None, :]
    cosine = jnp.cos(angle)[:, None, :]
    sine = jnp.sin(angle)[:, None, :]
    shaped = values.reshape(values.shape[:-1] + (heads, head_dim))
    first = shaped[..., :half]
    second = shaped[..., half:]
    turned = jnp.concatenate(
        [first * cosine - second * sine, first * sine + second * cosine], axis=-1
    )
    return turned.reshape(values.shape)


def body(
    state_tokens,
    gain_time,
    query_time,
    key_time,
    value_time,
    output_time,
    gain_space,
    query_space,
    key_space,
    value_space,
    output_space,
    neighbours,
):
    frames_here, tokens_here, features = state_tokens.shape
    head_dim = features // HEADS
    score_scale = 1.0 / jnp.sqrt(jnp.float32(head_dim))
    frame_count = lax.axis_size("frame")
    normed = rms_scale(state_tokens, gain_time)
    split_rows = normed.reshape(frames_here, frame_count, tokens_here // frame_count, features)
    shard_rows = lax.all_to_all(split_rows, "frame", split_axis=1, concat_axis=0, tiled=True)
    frames, unused_one, item_count, unused_width = shard_rows.shape
    flat_rows = shard_rows.reshape(frames, item_count, features)
    t_query = (
        project_rows(flat_rows, query_time)
        .astype(jnp.bfloat16)
        .reshape(frames, item_count, HEADS, head_dim)
    )
    t_key = (
        project_rows(flat_rows, key_time)
        .astype(jnp.bfloat16)
        .reshape(frames, item_count, HEADS, head_dim)
    )
    t_value = (
        project_rows(flat_rows, value_time)
        .astype(jnp.bfloat16)
        .reshape(frames, item_count, HEADS, head_dim)
    )
    scores = (
        jnp.einsum("fghd,eghd->ghfe", t_query, t_key, preferred_element_type=jnp.float32)
        * score_scale
    )
    weights = jax.nn.softmax(scores, axis=-1).astype(jnp.bfloat16)
    result = jnp.einsum("ghfe,eghd->fghd", weights, t_value, preferred_element_type=jnp.float32)
    gathered = result.astype(jnp.bfloat16).reshape(frames, 1, item_count, features)
    returned = lax.all_to_all(gathered, "frame", split_axis=0, concat_axis=1, tiled=True)
    returned = returned.reshape(frames_here, tokens_here, features)
    middle = (state_tokens.astype(jnp.float32) + project_rows(returned, output_time)).astype(
        jnp.bfloat16
    )
    normed_space = rms_scale(middle, gain_space)
    tile_place = lax.axis_index("tile")
    tile_count = lax.axis_size("tile")
    token_total = tile_count * tokens_here
    own_positions = tile_place * tokens_here + jnp.arange(tokens_here, dtype=jnp.int32)
    space_query = rotate_pairs(
        project_rows(normed_space, query_space), own_positions, HEADS
    ).astype(jnp.bfloat16)
    wide_rows = padded(normed_space, (("tile", 1),), tokens_here)
    wide_positions = (
        (tile_place - 1) * tokens_here + jnp.arange(3 * tokens_here, dtype=jnp.int32)
    ) % token_total
    space_key = rotate_pairs(project_rows(wide_rows, key_space), wide_positions, HEADS).astype(
        jnp.bfloat16
    )
    space_value = project_rows(wide_rows, value_space).astype(jnp.bfloat16)
    local_blocks = tokens_here // BLOCK
    block_total = local_blocks * tile_count
    group_count = local_blocks // 4
    valid_slot = neighbours >= 0
    local_ids = (neighbours - (tile_place - 1) * local_blocks) % block_total
    local_ids = jnp.where(valid_slot, local_ids, 0)
    key_blocks = space_key.reshape(frames_here, 3 * local_blocks, BLOCK, features)
    value_blocks = space_value.reshape(frames_here, 3 * local_blocks, BLOCK, features)
    query_blocks = space_query.reshape(frames_here, group_count, 4, BLOCK, features)
    id_groups = local_ids.reshape(group_count, 4, NEIGHBOUR_COUNT)
    slot_groups = valid_slot.reshape(group_count, 4, NEIGHBOUR_COUNT)

    def attend_group(group_index):
        query = query_blocks[:, group_index]
        block_ids = id_groups[group_index]
        gathered_keys = key_blocks[:, block_ids].reshape(
            frames_here, 4, NEIGHBOUR_COUNT * BLOCK, features
        )
        gathered_values = value_blocks[:, block_ids].reshape(
            frames_here, 4, NEIGHBOUR_COUNT * BLOCK, features
        )
        key_mask = jnp.repeat(slot_groups[group_index], BLOCK, axis=1)
        head_outs = []
        for head_index in range(HEADS):
            lower = head_index * head_dim
            upper = lower + head_dim
            scores = (
                jnp.einsum(
                    "fbqd,fbkd->fbqk",
                    query[..., lower:upper],
                    gathered_keys[..., lower:upper],
                    preferred_element_type=jnp.float32,
                )
                * score_scale
            )
            scores = jnp.where(key_mask[None, :, None, :], scores, -1e30)
            weights = jax.nn.softmax(scores, axis=-1).astype(jnp.bfloat16)
            result = jnp.einsum(
                "fbqk,fbkd->fbqd",
                weights,
                gathered_values[..., lower:upper],
                preferred_element_type=jnp.float32,
            )
            head_outs.append(result.astype(jnp.bfloat16))
        return jnp.concatenate(head_outs, axis=-1)

    attended = lax.map(attend_group, jnp.arange(group_count, dtype=jnp.int32))
    attended = jnp.moveaxis(attended, 0, 1).reshape(frames_here, tokens_here, features)
    return (middle.astype(jnp.float32) + project_rows(attended, output_space)).astype(jnp.bfloat16)


def solution(mesh):
    return jax.shard_map(
        body,
        mesh=mesh,
        in_specs=(
            P("frame", "tile", None),
            P(),
            P(),
            P(),
            P(),
            P(),
            P(),
            P(),
            P(),
            P(),
            P(),
            P("tile", None),
        ),
        out_specs=P("frame", "tile", None),
        check_vma=False,
    )
```

profile of v0, /device:TPU:0, one launch (start us, length us, event | category | flops | bytes accessed | tf_op | source)
XLA Modules:
  0.0 799.4 jit_solution(17084526639335226368)
XLA Ops:
  4.5 29.8 %all_to_all.30 = bf16[4,4,256,256]{3,2,0,1:T(8,128)(2,1)S(1)} all-to-all(bf16[4,4,256,256]{3,2,0,1:T(8,128)(2,1)S(1)} %copy.79), channel_id=1, replica_groups=mesh['frame'=4,'tile'=8] {'frame'}, dimensions={1} | all-to-all | bytes 4194304 | tf_op jit(solution)/shard_map/all_to_all | solution.py:77
  36.4 12.6 %copy.85 = bf16[16,256,8,32]{3,0,2,1:T(8,128)(2,1)} copy(bf16[16,256,8,32]{1,3,2,0:T(8,128)(2,1)} %bitcast.179) | data formatting | bytes 4194304 | tf_op jit(solution)/shard_map/reshape | solution.py:93
  51.1 12.6 %copy.83 = bf16[16,256,8,32]{3,0,2,1:T(8,128)(2,1)} copy(bf16[16,256,8,32]{1,3,2,0:T(8,128)(2,1)} %bitcast.180) | data formatting | bytes 4194304 | tf_op jit(solution)/shard_map/reshape | solution.py:83
  65.7 12.6 %copy.84 = bf16[16,256,8,32]{3,0,2,1:T(8,128)(2,1)} copy(bf16[16,256,8,32]{1,3,2,0:T(8,128)(2,1)} %bitcast.178) | data formatting | bytes 4194304 | tf_op jit(solution)/shard_map/reshape | solution.py:88
  78.3 14.8 %fusion.329 = (f32[256,8,16]{2,1,0:T(8,128)S(1)}, f32[256,8,16,16]{2,3,1,0:T(8,128)}) fusion(bf16[16,256,8,32]{3,0,2,1:T(8,128)(2,1)} %copy.83, bf16[16,256,8,32]{3,0,2,1:T(8,128)(2,1)} %copy.84), kind=kOutput, calls=%fused_computation.258 | convolution fusion | flops 35127312 | bytes 6422528 | tf_op jit(solution)/shard_map/sub | solution.py:99
  93.1 13.1 %convert_bitcast_fusion = bf16[16,256,8,32]{3,0,2,1:T(8,128)(2,1)} fusion(bf16[16,256,8,32]{3,0,2,1:T(8,128)(2,1)} %copy.85, f32[256,8,16,16]{2,3,1,0:T(8,128)} %get-tuple-element.97, f32[256,8,16]{2,1,0:T(8,128)S(1)} %get-tuple-element.96), kind=kOutput, calls=%fused_computation.176 | convolution fusion | flops 35651584 | bytes 6422528 | tf_op jit(solution)/shard_map/ghfe,eghd->fghd/dot_general | solution.py:100
  106.2 10.3 %copy.87 = bf16[16,256,8,32]{1,3,2,0:T(8,128)(2,1)} copy(bf16[16,256,8,32]{3,0,2,1:T(8,128)(2,1)} %convert_bitcast_fusion) | data formatting | bytes 4194304 | tf_op jit(solution)/shard_map/convert_element_type | solution.py:101
  121.6 25.4 %all-to-all-done.1 = bf16[16,1,256,256]{2,3,1,0:T(8,128)(2,1)} async-done(((bf16[16,1,256,256]{2,3,1,0:T(8,128)(2,1)}), bf16[16,1,256,256]{2,3,1,0:T(8,128)(2,1)}, u32[]{:S(2)}, u32[]{:S(2)}) %all-to-all-start.1) | async-done | bytes 2097184 | tf_op jit(solution)/shard_map/all_to_all | solution.py:102
  167.6 79.1 %collective-permute-done.1 = bf16[4,1024,256]{2,1,0:T(8,128)(2,1)} collective-permute-done((bf16[4,1024,256]{2,1,0:T(8,128)(2,1)S(1)}, bf16[4,1024,256]{2,1,0:T(8,128)(2,1)}, u32[]{:S(2)}, u32[]{:S(2)}) %collective-permute-start.1) | collective-permute-done | bytes 2097184 | tf_op jit(solution)/shard_map/ppermute | solution.py:23
  260.5 9.1 %copy.94 = bf16[4,24,128,256]{3,2,1,0:T(8,128)(2,1)} copy(bf16[4,24,128,256]{2,1,3,0:T(8,128)(2,1)} %bitcast.177) | data formatting | bytes 12582912 | tf_op jit(solution)/shard_map/while | solution.py:169
  274.7 519.8 %while.10 = (s32[]{:T(128)}, bf16[2,4,4,128,256]{4,3,2,0,1:T(8,128)(2,1)}, s32[2]{0:T(128)S(1)}, pred[2,4,9]{2,1,0:T(4,128)(4,1)S(1)}, bf16[4,2,4,128,256]{3,2,1...) while((s32[]{:T(128)}, ...), condition=%wide.region_21.22_spmd, body=%wide.region_4.21_spmd.sunk | while | flops 3794307584 | bytes 359888736 | solution.py:169
  278.0 8.2 %gather_fusion = bf16[36,4,128,256]{3,2,1,0:T(8,128)(2,1)} fusion(bf16[4,24,128,256]{3,2,1,0:T(8,128)(2,1)} %get-tuple-element.178, s32[1024]{0:T(1024)S(1)} %pad_clamp_fusion.2), kind=kCustom, calls=%fused_computation.1.clone.1 | custom fusion | bytes 18874512 | tf_op jit(solution)/shard_map/while/body/eval_jaxpr/gather | solution.py:141
  286.2 8.7 %copy.135 = bf16[36,4,128,256]{3,2,0,1:T(8,128)(2,1)} copy(bf16[36,4,128,256]{3,2,1,0:T(8,128)(2,1)} %gather_fusion) | data formatting | bytes 18874368 | tf_op jit(solution)/shard_map/while/body/eval_jaxpr/gather | solution.py:141
  295.0 8.5 %gather_fusion.1 = bf16[36,4,128,256]{3,2,1,0:T(8,128)(2,1)} fusion(bf16[4,24,128,256]{3,2,1,0:T(8,128)(2,1)} %get-tuple-element.177, s32[1024]{0:T(1024)S(1)} %pad_clamp_fusion.2), kind=kCustom, calls=%fused_computation.clone.1 | custom fusion | bytes 18874512 | tf_op jit(solution)/shard_map/while/body/eval_jaxpr/gather | solution.py:138
  303.5 8.9 %copy.137 = bf16[36,4,128,256]{3,2,0,1:T(8,128)(2,1)} copy(bf16[36,4,128,256]{3,2,1,0:T(8,128)(2,1)} %gather_fusion.1) | data formatting | bytes 18874368 | tf_op jit(solution)/shard_map/while/body/eval_jaxpr/gather | solution.py:138
  318.6 7.7 fusion.449
  326.3 10.5 %fusion.450 = bf16[4,4,128,256]{2,3,1,0:T(8,128)(2,1)S(1)} fusion(bf16[4,4,1152,256]{3,2,1,0:T(8,128)(2,1)} %bitcast.148, f32[4,4,128]{2,1,0:T(4,128)S(1)} %fusion.448, f32[4,4,128,1152]{3,2,1,0:T(8,128)} %fusion.449, pred[4,1152]{1,0:T(4,128)(4,1)S(1)} %bitcast.188), kind=kOutput, calls=%fused_computation.113.clone.1 | convolution fusion | flops 162860160 | bytes 14299648 | tf_op jit(solution)/shard_map/while/body/eval_jaxpr/fbqk,fbkd->fbqd/dot_general | solution.py:160
  344.1 8.5 %fusion.452 = f32[4,4,128,1152]{3,2,1,0:T(8,128)} fusion(bf16[4,4,1152,256]{3,2,1,0:T(8,128)(2,1)} %bitcast.134, bf16[4,4,128,256]{2,3,1,0:T(8,128)(2,1)S(1)} %bitcast.159), kind=kOutput, calls=%fused_computation.68.clone.2 | convolution fusion | flops 150994944 | bytes 14286848 | tf_op jit(solution)/shard_map/while/body/eval_jaxpr/fbqd,fbkd->fbqk/dot_general | solution.py:150
  352.6 13.1 %fusion.453 = bf16[4,4,128,256]{2,3,1,0:T(8,128)(2,1)S(1)} fusion(bf16[4,4,128,256]{2,3,1,0:T(8,128)(2,1)S(1)} %fusion.450, bf16[4,4,1152,256]{3,2,1,0:T(8,128)(2,1)} %bitcast.149, f32[4,4,128]{2,1,0:T(4,128)S(1)} %fusion.451, f32[4,4,128,1152]{3,2,1,0:T(8,128)} %fusion.452, pred[4,1152]{1,0:T(4,128)(4,1)S(1)} %bitcast.190), kind=kOutput, calls=%fused_computation.112.clone.1 | convolution fusion | flops 162860160 | bytes 14299648 | tf_op jit(solution)/shard_map/while/body/eval_jaxpr/fbqk,fbkd->fbqd/dot_general | solution.py:160
  372.8 8.5 %fusion.455 = f32[4,4,128,1152]{3,2,1,0:T(8,128)} fusion(bf16[4,4,1152,256]{3,2,1,0:T(8,128)(2,1)} %bitcast.136, bf16[4,4,128,256]{2,3,1,0:T(8,128)(2,1)S(1)} %bitcast.161), kind=kOutput, calls=%fused_computation.64.clone.2 | convolution fusion | flops 150994944 | bytes 14286848 | tf_op jit(solution)/shard_map/while/body/eval_jaxpr/fbqd,fbkd->fbqk/dot_general | solution.py:150
  381.3 12.9 %fusion.456 = bf16[4,4,128,256]{2,3,1,0:T(8,128)(2,1)S(1)} fusion(bf16[4,4,128,256]{2,3,1,0:T(8,128)(2,1)S(1)} %fusion.453, bf16[4,4,1152,256]{3,2,1,0:T(8,128)(2,1)} %bitcast.150, f32[4,4,128]{2,1,0:T(4,128)S(1)} %fusion.454, f32[4,4,128,1152]{3,2,1,0:T(8,128)} %fusion.455, pred[4,1152]{1,0:T(4,128)(4,1)S(1)} %bitcast.192), kind=kOutput, calls=%fused_computation.111.clone.1 | convolution fusion | flops 162860160 | bytes 14299648 | tf_op jit(solution)/shard_map/while/body/eval_jaxpr/fbqk,fbkd->fbqd/dot_general | solution.py:160
  401.3 8.5 %fusion.458 = f32[4,4,128,1152]{3,2,1,0:T(8,128)} fusion(bf16[4,4,1152,256]{3,2,1,0:T(8,128)(2,1)} %bitcast.138, bf16[4,4,128,256]{2,3,1,0:T(8,128)(2,1)S(1)} %bitcast.163), kind=kOutput, calls=%fused_computation.60.clone.2 | convolution fusion | flops 150994944 | bytes 14286848 | tf_op jit(solution)/shard_map/while/body/eval_jaxpr/fbqd,fbkd->fbqk/dot_general | solution.py:150
  409.7 12.9 %fusion.459 = bf16[4,4,128,256]{2,3,1,0:T(8,128)(2,1)S(1)} fusion(bf16[4,4,128,256]{2,3,1,0:T(8,128)(2,1)S(1)} %fusion.456, bf16[4,4,1152,256]{3,2,1,0:T(8,128)(2,1)} %bitcast.151, f32[4,4,128]{2,1,0:T(4,128)S(1)} %fusion.457, f32[4,4,128,1152]{3,2,1,0:T(8,128)} %fusion.458, pred[4,1152]{1,0:T(4,128)(4,1)S(1)} %bitcast.194), kind=kOutput, calls=%fused_computation.110.clone.1 | convolution fusion | flops 162860160 | bytes 14299648 | tf_op jit(solution)/shard_map/while/body/eval_jaxpr/fbqk,fbkd->fbqd/dot_general | solution.py:160
  436.0 10.9 %fusion.462 = bf16[4,4,128,256]{2,3,1,0:T(8,128)(2,1)S(1)} fusion(bf16[4,4,128,256]{2,3,1,0:T(8,128)(2,1)S(1)} %fusion.459, bf16[4,4,1152,256]{3,2,1,0:T(8,128)(2,1)} %bitcast.152, f32[4,4,128]{2,1,0:T(4,128)S(1)} %fusion.460, f32[4,4,128,1152]{3,2,1,0:T(8,128)} %fusion.461, pred[4,1152]{1,0:T(4,128)(4,1)S(1)} %bitcast.196), kind=kOutput, calls=%fused_computation.109.clone.1 | convolution fusion | flops 162860160 | bytes 14299648 | tf_op jit(solution)/shard_map/while/body/eval_jaxpr/fbqk,fbkd->fbqd/dot_general | solution.py:160
  454.0 8.5 %fusion.464 = f32[4,4,128,1152]{3,2,1,0:T(8,128)} fusion(bf16[4,4,1152,256]{3,2,1,0:T(8,128)(2,1)} %bitcast.142, bf16[4,4,128,256]{2,3,1,0:T(8,128)(2,1)S(1)} %bitcast.167), kind=kOutput, calls=%fused_computation.52.clone.2 | convolution fusion | flops 150994944 | bytes 14286848 | tf_op jit(solution)/shard_map/while/body/eval_jaxpr/fbqd,fbkd->fbqk/dot_general | solution.py:150
  462.5 12.8 %fusion.465 = bf16[4,4,128,256]{2,3,1,0:T(8,128)(2,1)S(1)} fusion(bf16[4,4,128,256]{2,3,1,0:T(8,128)(2,1)S(1)} %fusion.462, bf16[4,4,1152,256]{3,2,1,0:T(8,128)(2,1)} %bitcast.153, f32[4,4,128]{2,1,0:T(4,128)S(1)} %fusion.463, f32[4,4,128,1152]{3,2,1,0:T(8,128)} %fusion.464, pred[4,1152]{1,0:T(4,128)(4,1)S(1)} %bitcast.198), kind=kOutput, calls=%fused_computation.108.clone.1 | convolution fusion | flops 162860160 | bytes 14299648 | tf_op jit(solution)/shard_map/while/body/eval_jaxpr/fbqk,fbkd->fbqd/dot_general | solution.py:160
  482.4 8.5 %fusion.467 = f32[4,4,128,1152]{3,2,1,0:T(8,128)} fusion(bf16[4,4,1152,256]{3,2,1,0:T(8,128)(2,1)} %bitcast.144, bf16[4,4,128,256]{2,3,1,0:T(8,128)(2,1)S(1)} %bitcast.169), kind=kOutput, calls=%fused_computation.48.clone.2 | convolution fusion | flops 150994944 | bytes 14286848 | tf_op jit(solution)/shard_map/while/body/eval_jaxpr/fbqd,fbkd->fbqk/dot_general | solution.py:150
  490.9 12.9 %fusion.468 = bf16[4,4,128,256]{2,3,1,0:T(8,128)(2,1)S(1)} fusion(bf16[4,4,128,256]{2,3,1,0:T(8,128)(2,1)S(1)} %fusion.465, bf16[4,4,1152,256]{3,2,1,0:T(8,128)(2,1)} %bitcast.154, f32[4,4,128]{2,1,0:T(4,128)S(1)} %fusion.466, f32[4,4,128,1152]{3,2,1,0:T(8,128)} %fusion.467, pred[4,1152]{1,0:T(4,128)(4,1)S(1)} %bitcast.200), kind=kOutput, calls=%fused_computation.107.clone.1 | convolution fusion | flops 162860160 | bytes 14299648 | tf_op jit(solution)/shard_map/while/body/eval_jaxpr/fbqk,fbkd->fbqd/dot_general | solution.py:160
  510.9 8.5 %fusion.470 = f32[4,4,128,1152]{3,2,1,0:T(8,128)} fusion(bf16[4,4,1152,256]{3,2,1,0:T(8,128)(2,1)} %bitcast.146, bf16[4,4,128,256]{2,3,1,0:T(8,128)(2,1)S(1)} %bitcast.171), kind=kOutput, calls=%fused_computation.44.clone.2 | convolution fusion | flops 150994944 | bytes 14286848 | tf_op jit(solution)/shard_map/while/body/eval_jaxpr/fbqd,fbkd->fbqk/dot_general | solution.py:150
  519.3 12.9 %fusion.471 = bf16[4,4,128,256]{2,3,1,0:T(8,128)(2,1)S(1)} fusion(bf16[4,4,128,256]{2,3,1,0:T(8,128)(2,1)S(1)} %fusion.468, bf16[4,4,1152,256]{3,2,1,0:T(8,128)(2,1)} %bitcast.155, f32[4,4,128]{2,1,0:T(4,128)S(1)} %fusion.469, f32[4,4,128,1152]{3,2,1,0:T(8,128)} %fusion.470, pred[4,1152]{1,0:T(4,128)(4,1)S(1)} %bitcast.202), kind=kOutput, calls=%fused_computation.106.clone.1 | convolution fusion | flops 162860160 | bytes 14299648 | tf_op jit(solution)/shard_map/while/body/eval_jaxpr/fbqk,fbkd->fbqd/dot_general | solution.py:160
  537.2 8.2 %gather_fusion = bf16[36,4,128,256]{3,2,1,0:T(8,128)(2,1)} fusion(bf16[4,24,128,256]{3,2,1,0:T(8,128)(2,1)} %get-tuple-element.178, s32[1024]{0:T(1024)S(1)} %pad_clamp_fusion.2), kind=kCustom, calls=%fused_computation.1.clone.1 | custom fusion | bytes 18874512 | tf_op jit(solution)/shard_map/while/body/eval_jaxpr/gather | solution.py:141
  545.4 8.7 %copy.135 = bf16[36,4,128,256]{3,2,0,1:T(8,128)(2,1)} copy(bf16[36,4,128,256]{3,2,1,0:T(8,128)(2,1)} %gather_fusion) | data formatting | bytes 18874368 | tf_op jit(solution)/shard_map/while/body/eval_jaxpr/gather | solution.py:141
  554.2 8.4 %gather_fusion.1 = bf16[36,4,128,256]{3,2,1,0:T(8,128)(2,1)} fusion(bf16[4,24,128,256]{3,2,1,0:T(8,128)(2,1)} %get-tuple-element.177, s32[1024]{0:T(1024)S(1)} %pad_clamp_fusion.2), kind=kCustom, calls=%fused_computation.clone.1 | custom fusion | bytes 18874512 | tf_op jit(solution)/shard_map/while/body/eval_jaxpr/gather | solution.py:138
  562.6 8.9 %copy.137 = bf16[36,4,128,256]{3,2,0,1:T(8,128)(2,1)} copy(bf16[36,4,128,256]{3,2,1,0:T(8,128)(2,1)} %gather_fusion.1) | data formatting | bytes 18874368 | tf_op jit(solution)/shard_map/while/body/eval_jaxpr/gather | solution.py:138
  585.4 10.5 %fusion.450 = bf16[4,4,128,256]{2,3,1,0:T(8,128)(2,1)S(1)} fusion(bf16[4,4,1152,256]{3,2,1,0:T(8,128)(2,1)} %bitcast.148, f32[4,4,128]{2,1,0:T(4,128)S(1)} %fusion.448, f32[4,4,128,1152]{3,2,1,0:T(8,128)} %fusion.449, pred[4,1152]{1,0:T(4,128)(4,1)S(1)} %bitcast.188), kind=kOutput, calls=%fused_computation.113.clone.1 | convolution fusion | flops 162860160 | bytes 14299648 | tf_op jit(solution)/shard_map/while/body/eval_jaxpr/fbqk,fbkd->fbqd/dot_general | solution.py:160
  603.3 8.5 %fusion.452 = f32[4,4,128,1152]{3,2,1,0:T(8,128)} fusion(bf16[4,4,1152,256]{3,2,1,0:T(8,128)(2,1)} %bitcast.134, bf16[4,4,128,256]{2,3,1,0:T(8,128)(2,1)S(1)} %bitcast.159), kind=kOutput, calls=%fused_computation.68.clone.2 | convolution fusion | flops 150994944 | bytes 14286848 | tf_op jit(solution)/shard_map/while/body/eval_jaxpr/fbqd,fbkd->fbqk/dot_general | solution.py:150
  611.7 13.1 %fusion.453 = bf16[4,4,128,256]{2,3,1,0:T(8,128)(2,1)S(1)} fusion(bf16[4,4,128,256]{2,3,1,0:T(8,128)(2,1)S(1)} %fusion.450, bf16[4,4,1152,256]{3,2,1,0:T(8,128)(2,1)} %bitcast.149, f32[4,4,128]{2,1,0:T(4,128)S(1)} %fusion.451, f32[4,4,128,1152]{3,2,1,0:T(8,128)} %fusion.452, pred[4,1152]{1,0:T(4,128)(4,1)S(1)} %bitcast.190), kind=kOutput, calls=%fused_computation.112.clone.1 | convolution fusion | flops 162860160 | bytes 14299648 | tf_op jit(solution)/shard_map/while/body/eval_jaxpr/fbqk,fbkd->fbqd/dot_general | solution.py:160
  632.0 8.5 %fusion.455 = f32[4,4,128,1152]{3,2,1,0:T(8,128)} fusion(bf16[4,4,1152,256]{3,2,1,0:T(8,128)(2,1)} %bitcast.136, bf16[4,4,128,256]{2,3,1,0:T(8,128)(2,1)S(1)} %bitcast.161), kind=kOutput, calls=%fused_computation.64.clone.2 | convolution fusion | flops 150994944 | bytes 14286848 | tf_op jit(solution)/shard_map/while/body/eval_jaxpr/fbqd,fbkd->fbqk/dot_general | solution.py:150
  640.4 12.9 %fusion.456 = bf16[4,4,128,256]{2,3,1,0:T(8,128)(2,1)S(1)} fusion(bf16[4,4,128,256]{2,3,1,0:T(8,128)(2,1)S(1)} %fusion.453, bf16[4,4,1152,256]{3,2,1,0:T(8,128)(2,1)} %bitcast.150, f32[4,4,128]{2,1,0:T(4,128)S(1)} %fusion.454, f32[4,4,128,1152]{3,2,1,0:T(8,128)} %fusion.455, pred[4,1152]{1,0:T(4,128)(4,1)S(1)} %bitcast.192), kind=kOutput, calls=%fused_computation.111.clone.1 | convolution fusion | flops 162860160 | bytes 14299648 | tf_op jit(solution)/shard_map/while/body/eval_jaxpr/fbqk,fbkd->fbqd/dot_general | solution.py:160
  660.4 8.5 %fusion.458 = f32[4,4,128,1152]{3,2,1,0:T(8,128)} fusion(bf16[4,4,1152,256]{3,2,1,0:T(8,128)(2,1)} %bitcast.138, bf16[4,4,128,256]{2,3,1,0:T(8,128)(2,1)S(1)} %bitcast.163), kind=kOutput, calls=%fused_computation.60.clone.2 | convolution fusion | flops 150994944 | bytes 14286848 | tf_op jit(solution)/shard_map/while/body/eval_jaxpr/fbqd,fbkd->fbqk/dot_general | solution.py:150
  668.9 12.9 %fusion.459 = bf16[4,4,128,256]{2,3,1,0:T(8,128)(2,1)S(1)} fusion(bf16[4,4,128,256]{2,3,1,0:T(8,128)(2,1)S(1)} %fusion.456, bf16[4,4,1152,256]{3,2,1,0:T(8,128)(2,1)} %bitcast.151, f32[4,4,128]{2,1,0:T(4,128)S(1)} %fusion.457, f32[4,4,128,1152]{3,2,1,0:T(8,128)} %fusion.458, pred[4,1152]{1,0:T(4,128)(4,1)S(1)} %bitcast.194), kind=kOutput, calls=%fused_computation.110.clone.1 | convolution fusion | flops 162860160 | bytes 14299648 | tf_op jit(solution)/shard_map/while/body/eval_jaxpr/fbqk,fbkd->fbqd/dot_general | solution.py:160
  695.2 10.9 %fusion.462 = bf16[4,4,128,256]{2,3,1,0:T(8,128)(2,1)S(1)} fusion(bf16[4,4,128,256]{2,3,1,0:T(8,128)(2,1)S(1)} %fusion.459, bf16[4,4,1152,256]{3,2,1,0:T(8,128)(2,1)} %bitcast.152, f32[4,4,128]{2,1,0:T(4,128)S(1)} %fusion.460, f32[4,4,128,1152]{3,2,1,0:T(8,128)} %fusion.461, pred[4,1152]{1,0:T(4,128)(4,1)S(1)} %bitcast.196), kind=kOutput, calls=%fused_computation.109.clone.1 | convolution fusion | flops 162860160 | bytes 14299648 | tf_op jit(solution)/shard_map/while/body/eval_jaxpr/fbqk,fbkd->fbqd/dot_general | solution.py:160
  713.2 8.5 %fusion.464 = f32[4,4,128,1152]{3,2,1,0:T(8,128)} fusion(bf16[4,4,1152,256]{3,2,1,0:T(8,128)(2,1)} %bitcast.142, bf16[4,4,128,256]{2,3,1,0:T(8,128)(2,1)S(1)} %bitcast.167), kind=kOutput, calls=%fused_computation.52.clone.2 | convolution fusion | flops 150994944 | bytes 14286848 | tf_op jit(solution)/shard_map/while/body/eval_jaxpr/fbqd,fbkd->fbqk/dot_general | solution.py:150
  721.6 12.8 %fusion.465 = bf16[4,4,128,256]{2,3,1,0:T(8,128)(2,1)S(1)} fusion(bf16[4,4,128,256]{2,3,1,0:T(8,128)(2,1)S(1)} %fusion.462, bf16[4,4,1152,256]{3,2,1,0:T(8,128)(2,1)} %bitcast.153, f32[4,4,128]{2,1,0:T(4,128)S(1)} %fusion.463, f32[4,4,128,1152]{3,2,1,0:T(8,128)} %fusion.464, pred[4,1152]{1,0:T(4,128)(4,1)S(1)} %bitcast.198), kind=kOutput, calls=%fused_computation.108.clone.1 | convolution fusion | flops 162860160 | bytes 14299648 | tf_op jit(solution)/shard_map/while/body/eval_jaxpr/fbqk,fbkd->fbqd/dot_general | solution.py:160
  741.6 8.5 %fusion.467 = f32[4,4,128,1152]{3,2,1,0:T(8,128)} fusion(bf16[4,4,1152,256]{3,2,1,0:T(8,128)(2,1)} %bitcast.144, bf16[4,4,128,256]{2,3,1,0:T(8,128)(2,1)S(1)} %bitcast.169), kind=kOutput, calls=%fused_computation.48.clone.2 | convolution fusion | flops 150994944 | bytes 14286848 | tf_op jit(solution)/shard_map/while/body/eval_jaxpr/fbqd,fbkd->fbqk/dot_general | solution.py:150
  750.0 12.9 %fusion.468 = bf16[4,4,128,256]{2,3,1,0:T(8,128)(2,1)S(1)} fusion(bf16[4,4,128,256]{2,3,1,0:T(8,128)(2,1)S(1)} %fusion.465, bf16[4,4,1152,256]{3,2,1,0:T(8,128)(2,1)} %bitcast.154, f32[4,4,128]{2,1,0:T(4,128)S(1)} %fusion.466, f32[4,4,128,1152]{3,2,1,0:T(8,128)} %fusion.467, pred[4,1152]{1,0:T(4,128)(4,1)S(1)} %bitcast.200), kind=kOutput, calls=%fused_computation.107.clone.1 | convolution fusion | flops 162860160 | bytes 14299648 | tf_op jit(solution)/shard_map/while/body/eval_jaxpr/fbqk,fbkd->fbqd/dot_general | solution.py:160
  770.0 8.5 %fusion.470 = f32[4,4,128,1152]{3,2,1,0:T(8,128)} fusion(bf16[4,4,1152,256]{3,2,1,0:T(8,128)(2,1)} %bitcast.146, bf16[4,4,128,256]{2,3,1,0:T(8,128)(2,1)S(1)} %bitcast.171), kind=kOutput, calls=%fused_computation.44.clone.2 | convolution fusion | flops 150994944 | bytes 14286848 | tf_op jit(solution)/shard_map/while/body/eval_jaxpr/fbqd,fbkd->fbqk/dot_general | solution.py:150
  778.5 12.9 %fusion.471 = bf16[4,4,128,256]{2,3,1,0:T(8,128)(2,1)S(1)} fusion(bf16[4,4,128,256]{2,3,1,0:T(8,128)(2,1)S(1)} %fusion.468, bf16[4,4,1152,256]{3,2,1,0:T(8,128)(2,1)} %bitcast.155, f32[4,4,128]{2,1,0:T(4,128)S(1)} %fusion.469, f32[4,4,128,1152]{3,2,1,0:T(8,128)} %fusion.470, pred[4,1152]{1,0:T(4,128)(4,1)S(1)} %bitcast.202), kind=kOutput, calls=%fused_computation.106.clone.1 | convolution fusion | flops 162860160 | bytes 14299648 | tf_op jit(solution)/shard_map/while/body/eval_jaxpr/fbqk,fbkd->fbqd/dot_general | solution.py:160
  (132 shorter events, 196.7 us)
Async XLA Ops:
  0.0 269.6 %copy-start = (bf16[256,256]{1,0:T(8,128)(2,1)S(1)}, bf16[256,256]{1,0:T(8,128)(2,1)}, u32[]{:S(2)}) copy-start(bf16[256,256]{1,0:T(8,128)(2,1)} %param.23) | copy-start | bytes 393220
  0.0 34.3 %copy-start.5 = (bf16[256,256]{1,0:T(8,128)(2,1)S(1)}, bf16[256,256]{1,0:T(8,128)(2,1)}, u32[]{:S(2)}) copy-start(bf16[256,256]{1,0:T(8,128)(2,1)} %param.18) | copy-start | bytes 393220
  4.5 44.5 %copy-start.6 = (bf16[256,256]{1,0:T(8,128)(2,1)S(1)}, bf16[256,256]{1,0:T(8,128)(2,1)}, u32[]{:S(2)}) copy-start(bf16[256,256]{1,0:T(8,128)(2,1)} %param.16) | copy-start | bytes 393220
  49.0 14.7 %copy-start.7 = (bf16[256,256]{1,0:T(8,128)(2,1)S(1)}, bf16[256,256]{1,0:T(8,128)(2,1)}, u32[]{:S(2)}) copy-start(bf16[256,256]{1,0:T(8,128)(2,1)} %param.17) | copy-start | bytes 393220
  106.2 15.1 %copy-start.9 = (bf16[256,256]{1,0:T(8,128)(2,1)S(1)}, bf16[256,256]{1,0:T(8,128)(2,1)}, u32[]{:S(2)}) copy-start(bf16[256,256]{1,0:T(8,128)(2,1)} %param.21) | copy-start | bytes 393220
  106.2 15.2 %copy-start.10 = (bf16[256,256]{1,0:T(8,128)(2,1)S(1)}, bf16[256,256]{1,0:T(8,128)(2,1)}, u32[]{:S(2)}) copy-start(bf16[256,256]{1,0:T(8,128)(2,1)} %param.22) | copy-start | bytes 393220
  106.2 15.4 %copy-start.13 = (s32[8,9]{1,0:T(8,128)S(1)}, s32[8,9]{1,0:T(8,128)}, u32[]{:S(2)}) copy-start(s32[8,9]{1,0:T(8,128)} %param.25) | copy-start | bytes 868
  106.2 46.5 %copy-start.4 = (bf16[4,1024,256]{2,1,0:T(8,128)(2,1)S(1)}, bf16[4,1024,256]{2,1,0:T(8,128)(2,1)}, u32[]{:S(2)}) copy-start(bf16[4,1024,256]{2,1,0:T(8,128)(2,1)} %param.14) | copy-start | bytes 6291460
  106.2 46.5 %copy-start.17 = (bf16[256,256]{1,0:T(8,128)(2,1)S(1)}, bf16[256,256]{1,0:T(8,128)(2,1)}, u32[]{:S(2)}) copy-start(bf16[256,256]{1,0:T(8,128)(2,1)} %param.19) | copy-start | bytes 393220
  116.5 37.2 %copy-start.14 = (f32[256]{0:T(256)S(1)}, f32[256]{0:T(256)}, u32[]{:S(2)}) copy-start(f32[256]{0:T(256)} %param.20) | copy-start | bytes 3076
  116.5 30.6 %all-to-all-start.1 = ((bf16[16,1,256,256]{2,3,1,0:T(8,128)(2,1)}), bf16[16,1,256,256]{2,3,1,0:T(8,128)(2,1)}, u32[]{:S(2)}, u32[]{:S(2)}) async-start(bf16[16,1,256,256]{2,3,1,0:T(8,128)(2,1)} %bitcast.29), calls=%async_computation.1 | async-start | bytes 4194304 | tf_op jit(solution)/shard_map/all_to_all | solution.py:102
  153.6 6.5 copy-start.3
  154.4 92.3 %collective-permute-start.1 = (bf16[4,1024,256]{2,1,0:T(8,128)(2,1)S(1)}, bf16[4,1024,256]{2,1,0:T(8,128)(2,1)}, u32[]{:S(2)}, u32[]{:S(2)}) collective-permute-start(bf16[4,1024,256]{2,1,0:T(8,128)(2,1)S(1)} %fusion.263), channel_id=1, source_target_pairs={{1,0},{2,1},{3,2},{4,3},{5,4},{6,5},{7,6},{0,7},{9,8},{10,9},{11,1... | collective-permute-start | bytes 6291464 | tf_op jit(solution)/shard_map/ppermute | solution.py:23
  159.0 87.7 %collective-permute-start = (bf16[4,1024,256]{2,1,0:T(8,128)(2,1)S(1)}, bf16[4,1024,256]{2,1,0:T(8,128)(2,1)}, u32[]{:S(2)}, u32[]{:S(2)}) collective-permute-start(bf16[4,1024,256]{2,1,0:T(8,128)(2,1)S(1)} %fusion.263), channel_id=1, source_target_pairs={{0,1},{1,2},{2,3},{3,4},{4,5},{5,6},{6,7},{7,0},{8,9},{9,10},{10,1... | collective-permute-start | bytes 6291464 | tf_op jit(solution)/shard_map/ppermute | solution.py:22
  274.7 519.9 %copy-start.8 = (bf16[256,256]{1,0:T(8,128)(2,1)S(1)}, bf16[256,256]{1,0:T(8,128)(2,1)}, u32[]{:S(2)}) copy-start(bf16[256,256]{1,0:T(8,128)(2,1)} %param.24) | copy-start | bytes 393220
  275.1 11.1 %copy-start.11 = (s32[2,4,9]{2,1,0:T(4,128)}, s32[2,4,9]{2,1,0:T(4,128)S(1)}, u32[]{:S(2)}) copy-start(s32[2,4,9]{2,1,0:T(4,128)S(1)} %get-tuple-element.176) | copy-start | bytes 868 | tf_op jit(solution)/shard_map/while
  275.1 11.1 %copy-start.18 = (s32[2]{0:T(128)}, s32[2]{0:T(128)S(1)}, u32[]{:S(2)}) copy-start(s32[2]{0:T(128)S(1)} %get-tuple-element.173) | copy-start | bytes 28 | tf_op jit(solution)/shard_map/while
  275.1 19.8 %copy-start.15 = (pred[2,4,9]{2,1,0:T(4,128)(4,1)}, pred[2,4,9]{2,1,0:T(4,128)(4,1)S(1)}, u32[]{:S(2)}) copy-start(pred[2,4,9]{2,1,0:T(4,128)(4,1)S(1)} %get-tuple-element.174) | copy-start | bytes 220 | tf_op jit(solution)/shard_map/while
  303.5 8.9 %copy-start.2 = (bf16[4,2,4,128,256]{3,2,1,4,0:T(4,128)(2,1)S(1)}, bf16[4,2,4,128,256]{3,2,1,4,0:T(4,128)(2,1)}, u32[]{:S(2)}) copy-start(bf16[4,2,4,128,256]{3,2,1,4,0:T(4,128)(2,1)} %get-tuple-element.175) | copy-start | bytes 6291460 | tf_op jit(solution)/shard_map/while
  519.3 14.5 %copy-start.12 = (s32[2,4,9]{2,1,0:T(4,128)S(1)}, s32[2,4,9]{2,1,0:T(4,128)}, u32[]{:S(2)}) copy-start(s32[2,4,9]{2,1,0:T(4,128)} %copy-done.11) | copy-start | bytes 868 | tf_op jit(solution)/shard_map/while
  519.3 14.5 %copy-start.16 = (pred[2,4,9]{2,1,0:T(4,128)(4,1)S(1)}, pred[2,4,9]{2,1,0:T(4,128)(4,1)}, u32[]{:S(2)}) copy-start(pred[2,4,9]{2,1,0:T(4,128)(4,1)} %copy-done.15) | copy-start | bytes 220 | tf_op jit(solution)/shard_map/while
  519.3 14.5 %copy-start.19 = (s32[2]{0:T(128)S(1)}, s32[2]{0:T(128)}, u32[]{:S(2)}) copy-start(s32[2]{0:T(128)} %copy-done.18) | copy-start | bytes 28 | tf_op jit(solution)/shard_map/while
  534.3 11.1 %copy-start.11 = (s32[2,4,9]{2,1,0:T(4,128)}, s32[2,4,9]{2,1,0:T(4,128)S(1)}, u32[]{:S(2)}) copy-start(s32[2,4,9]{2,1,0:T(4,128)S(1)} %get-tuple-element.176) | copy-start | bytes 868 | tf_op jit(solution)/shard_map/while
  534.3 11.1 %copy-start.18 = (s32[2]{0:T(128)}, s32[2]{0:T(128)S(1)}, u32[]{:S(2)}) copy-start(s32[2]{0:T(128)S(1)} %get-tuple-element.173) | copy-start | bytes 28 | tf_op jit(solution)/shard_map/while
  534.3 19.8 %copy-start.15 = (pred[2,4,9]{2,1,0:T(4,128)(4,1)}, pred[2,4,9]{2,1,0:T(4,128)(4,1)S(1)}, u32[]{:S(2)}) copy-start(pred[2,4,9]{2,1,0:T(4,128)(4,1)S(1)} %get-tuple-element.174) | copy-start | bytes 220 | tf_op jit(solution)/shard_map/while
  562.6 8.9 %copy-start.2 = (bf16[4,2,4,128,256]{3,2,1,4,0:T(4,128)(2,1)S(1)}, bf16[4,2,4,128,256]{3,2,1,4,0:T(4,128)(2,1)}, u32[]{:S(2)}) copy-start(bf16[4,2,4,128,256]{3,2,1,4,0:T(4,128)(2,1)} %get-tuple-element.175) | copy-start | bytes 6291460 | tf_op jit(solution)/shard_map/while
  778.5 14.5 %copy-start.12 = (s32[2,4,9]{2,1,0:T(4,128)S(1)}, s32[2,4,9]{2,1,0:T(4,128)}, u32[]{:S(2)}) copy-start(s32[2,4,9]{2,1,0:T(4,128)} %copy-done.11) | copy-start | bytes 868 | tf_op jit(solution)/shard_map/while
  778.5 14.5 %copy-start.16 = (pred[2,4,9]{2,1,0:T(4,128)(4,1)S(1)}, pred[2,4,9]{2,1,0:T(4,128)(4,1)}, u32[]{:S(2)}) copy-start(pred[2,4,9]{2,1,0:T(4,128)(4,1)} %copy-done.15) | copy-start | bytes 220 | tf_op jit(solution)/shard_map/while
  778.5 14.5 %copy-start.19 = (s32[2]{0:T(128)S(1)}, s32[2]{0:T(128)}, u32[]{:S(2)}) copy-start(s32[2]{0:T(128)} %copy-done.18) | copy-start | bytes 28 | tf_op jit(solution)/shard_map/while
  794.6 4.3 copy-start.1
where the time goes:
time: 811 us; the launch traced here: 799 us
  matrix products  487 us (60%)
  local copies, waits for them, and re-layouts  147 us (18%)
  waiting for transfers between devices  105 us (13%)
  blocking collectives  29.8 us (4%)
  other arithmetic  14 us (2%)
  starting transfers between devices  9.38 us (1%)
    dot_general x16, matrix products, attend_group(): jnp.einsum('fbqk,fbkd->fbqd', weights, gathered_values[..., lower:upper],...  198 us
    dot_general x16, matrix products, attend_group(): jnp.einsum('fbqd,fbkd->fbqk', query[..., lower:upper], gathered_keys[...,...  132 us
    sub x16, matrix products, attend_group(): weights = jax.nn.softmax(scores, axis=-1).astype(jnp.bfloat16)  108 us
    ppermute x1, waiting for transfers between devices, padded(): after = lax.ppermute(initial, axis, down)  79.1 us
    gather x4, local copies, waits for them, and re-layouts, attend_group(): key_blocks[:, block_ids]  34.6 us
    gather x4, local copies, waits for them, and re-layouts, attend_group(): value_blocks[:, block_ids]  33.8 us
    all_to_all x1, blocking collectives, body(): lax.all_to_all(split_rows, 'frame', split_axis=1, concat_axis=0, tiled=True)  29.8 us
    all_to_all x1, waiting for transfers between devices, body(): lax.all_to_all(gathered, 'frame', split_axis=0, concat_axis=1, tiled=True)  25.4 us
  transfers between devices with their start and end apart: 3, of which 2 were waited for; matrix products, arithmetic and copies ran while one was open for 1% of the time, Pallas kernels for 0%

commit v1 on v0

v1 whole, which is shorter than its diff:
```python
import functools

import jax
import jax.numpy as jnp
import numpy as np
from jax import lax
from jax.experimental import pallas as pl
from jax.experimental.pallas import tpu as pltpu
from jax.sharding import PartitionSpec as P

HEADS = 8
BLOCK = 128
NEIGHBOUR_COUNT = 9
EPS = 1e-05
ROT_PERIOD = 1024
LOG2E = 1.4426950408889634
SAFE_SCORE = 64.0
FRAME_CHUNKS = 4
BF16 = jnp.bfloat16
F32 = jnp.float32


def rms_rows(x, gain):
    square_mean = jnp.mean(x * x, axis=-1, keepdims=True)
    return (x * lax.rsqrt(square_mean + EPS) * gain).astype(BF16)


def mm(a, b):
    return jnp.dot(a, b, preferred_element_type=F32)


def mm_t(a, b):
    return lax.dot_general(a, b, (((1,), (1,)), ((), ())), preferred_element_type=F32)


def iota(shape, dim):
    return lax.broadcasted_iota(jnp.int32, shape, dim)


def time_kernel(scale, pieces, chunks, gain_ref, wq_ref, wk_ref, wv_ref, wo_ref, *refs):
    x_refs = refs[:pieces]
    o_refs = refs[pieces : pieces + pieces * chunks]
    q_s, k_s, v_s, a_s = refs[pieces + pieces * chunks :]
    tokens, width = x_refs[0].shape[1:]
    head_dim = width // HEADS
    frames = q_s.shape[0]
    x = jnp.concatenate([r[...].astype(F32) for r in x_refs], axis=0)
    normed = rms_rows(x, gain_ref[...]).reshape(frames * tokens, width)
    q_s[...] = (mm(normed, wq_ref[...]) * scale).reshape(frames, tokens, width)
    k_s[...] = mm(normed, wk_ref[...]).reshape(frames, tokens, width)
    v_s[...] = mm(normed, wv_ref[...]).reshape(frames, tokens, width)
    rows = frames * 8
    head_of = iota((1, width), 1) // head_dim
    same = (iota((rows, rows), 0) % 8) == (iota((rows, rows), 1) % 8)
    for g in range(tokens // 8):
        part = slice(g * 8, g * 8 + 8)
        q = q_s[:, part, :].reshape(rows, width)
        k = k_s[:, part, :].reshape(rows, width).astype(BF16)
        v = v_s[:, part, :].reshape(rows, width).astype(BF16)
        acc = None
        for h in range(HEADS):
            qm = jnp.where(head_of == h, q, 0.0).astype(BF16)
            s = jnp.where(same, mm_t(qm, k), -1e30)
            p = jnp.exp2(s - jnp.max(s, axis=1, keepdims=True))
            d = jnp.sum(p, axis=1, keepdims=True)
            o = mm(p.astype(BF16), v) / d
            acc = o if acc is None else jnp.where(head_of == h, o, acc)
        a_s[:, part, :] = acc.reshape(frames, 8, width)
    attended = a_s[...].reshape(frames * tokens, width).astype(BF16)
    middle = x + mm(attended, wo_ref[...]).reshape(frames, tokens, width)
    frames_here = x_refs[0].shape[0]
    step = frames_here // chunks
    for i in range(pieces):
        for j in range(chunks):
            low = i * frames_here + j * step
            o_refs[i * chunks + j][...] = middle[low : low + step].astype(BF16)


def time_stage(pieces, chunks, gain, wq, wk, wv, wo):
    frames_here, tokens, width = pieces[0].shape
    frames = frames_here * len(pieces)
    tile = min(tokens, 32)
    scale = LOG2E / float(np.sqrt(width // HEADS))
    full = pl.BlockSpec((width, width), lambda t: (0, 0))
    step = frames_here // chunks
    count = len(pieces) * chunks
    return pl.pallas_call(
        functools.partial(time_kernel, scale, len(pieces), chunks),
        grid=(tokens // tile,),
        in_specs=[pl.BlockSpec((1, width), lambda t: (0, 0))]
        + [full] * 4
        + [pl.BlockSpec((frames_here, tile, width), lambda t: (0, t, 0))] * len(pieces),
        out_specs=[pl.BlockSpec((step, tile, width), lambda t: (0, t, 0))] * count,
        out_shape=[jax.ShapeDtypeStruct((step, tokens, width), BF16)] * count,
        scratch_shapes=[pltpu.VMEM((frames, tile, width), F32)] * 4,
        compiler_params=pltpu.CompilerParams(vmem_limit_bytes=48 << 20),
        name="time_attention",
    )(gain, wq, wk, wv, wo, *pieces)


def space_kernel(scale, pieces, has_prev, ids, pos, gain_ref, wq_ref, wk_ref, wv_ref, wo_ref, cos_ref, sin_ref, *refs):
    x_refs = refs[: 3 * pieces]
    refs = refs[3 * pieces + (1 if has_prev else 0) :]
    o_ref, wq_s, wk_s, q_s, k_s, v_s, x_s, kg, vg, flag = refs
    frame, block = pl.program_id(0), pl.program_id(1)
    piece_rows, width = x_refs[0].shape[1:]
    half = width // 2
    head_dim = width // HEADS
    quarter = head_dim // 2

    @pl.when((frame == 0) & (block == 0))
    def _():
        src = iota((width, width), 0)
        dst = iota((width, width), 1)
        low = dst % half
        wanted = (low // quarter) * head_dim + low % quarter + jnp.where(dst >= half, quarter, 0)
        order = jnp.where(src == wanted, 1.0, 0.0).astype(BF16)
        wq_s[...] = mm(wq_ref[...], order).astype(BF16)
        wk_s[...] = mm(wk_ref[...], order).astype(BF16)

    @pl.when(block == 0)
    def _():
        same_head = jnp.where(
            iota((half, half), 0) // quarter == iota((half, half), 1) // quarter, 1.0, 0.0
        ).astype(BF16)

        def turn(rows, c, s):
            u, w = rows[:, :half], rows[:, half:]
            return u * c - w * s, u * s + w * c

        def head_squares(u, w):
            squares = mm((u * u + w * w).astype(BF16), same_head)
            return jnp.max(squares, axis=0, keepdims=True)

        k_top, q_top = None, None
        for side in range(3):
            for i in range(pieces):
                x_raw = x_refs[side * pieces + i][0]
                normed = rms_rows(x_raw.astype(F32), gain_ref[...])
                at = pl.ds(pl.multiple_of(pos[i], piece_rows), piece_rows)
                c, s = cos_ref[at, :], sin_ref[at, :]
                low = (side * pieces + i) * piece_rows
                rows = slice(low, low + piece_rows)
                u, w = turn(mm(normed, wk_s[...]), c, s)
                k_s[rows, :half] = u.astype(BF16)
                k_s[rows, half:] = w.astype(BF16)
                top = head_squares(u, w)
                k_top = top if k_top is None else jnp.maximum(k_top, top)
                v_s[rows, :] = mm(normed, wv_ref[...]).astype(BF16)
                if side == 0:
                    u, w = turn(mm(normed, wq_s[...]) * scale, c, s)
                    q_s[rows, :half] = u.astype(BF16)
                    q_s[rows, half:] = w.astype(BF16)
                    top = head_squares(u, w)
                    q_top = top if q_top is None else jnp.maximum(q_top, top)
                    x_s[rows, :] = x_raw
        flag[0] = jnp.max(k_top * q_top)

    for m in range(NEIGHBOUR_COUNT):
        at = pl.ds(pl.multiple_of(ids[block * (NEIGHBOUR_COUNT + 2) + m] * BLOCK, BLOCK), BLOCK)
        kg[m * BLOCK : (m + 1) * BLOCK, :] = k_s[at, :]
        vg[m * BLOCK : (m + 1) * BLOCK, :] = v_s[at, :]
    last = (NEIGHBOUR_COUNT - 1) * BLOCK
    present = ids[block * (NEIGHBOUR_COUNT + 2) + NEIGHBOUR_COUNT] > 0
    own = pl.ds(pl.multiple_of(ids[block * (NEIGHBOUR_COUNT + 2) + NEIGHBOUR_COUNT + 1] * BLOCK, BLOCK), BLOCK)
    lane = iota((1, width), 1)
    rot_head = (lane % half) // quarter
    head_of = lane // head_dim
    bias = jnp.where(present | (iota((1, NEIGHBOUR_COUNT * BLOCK), 1) < last), 0.0, -1e30)

    def attend(group, shift):
        q = q_s[own, :]
        acc = None
        for g in range(HEADS // group):
            heads = range(g * group, g * group + group)
            qm = jnp.concatenate([jnp.where(rot_head == h, q, 0).astype(BF16) for h in heads], axis=0)
            s = mm_t(qm, kg[...]) + bias
            if shift:
                s = s - jnp.max(s, axis=1, keepdims=True)
            p = jnp.exp2(s)
            d = jnp.sum(p, axis=1, keepdims=True)
            o = mm(p.astype(BF16), vg[...]) / d
            for j, h in enumerate(heads):
                part = o[j * BLOCK : (j + 1) * BLOCK]
                acc = part if acc is None else jnp.where(head_of == h, part, acc)
        y = mm(acc.astype(BF16), wo_ref[...])
        o_ref[0] = (x_s[own, :].astype(F32) + y).astype(BF16)

    safe = flag[0] <= SAFE_SCORE * SAFE_SCORE

    @pl.when(safe)
    def _():
        attend(4, False)

    @pl.when(jnp.logical_not(safe))
    def _():
        attend(2, True)


def space_stage(sides, ids, pos, gain, wq, wk, wv, wo, cos, sin, prev, chunk, chunks):
    pieces = len(sides[0])
    step, piece_rows, width = sides[0][0].shape
    tokens = pieces * piece_rows
    blocks = tokens // BLOCK
    scale = LOG2E / float(np.sqrt(width // HEADS))
    full = pl.BlockSpec((width, width), lambda f, b, *_: (0, 0))
    table = pl.BlockSpec(cos.shape, lambda f, b, *_: (0, 0))
    piece = pl.BlockSpec((1, piece_rows, width), lambda f, b, *_: (f, 0, 0))
    in_specs = [pl.BlockSpec((1, width), lambda f, b, *_: (0, 0))] + [full] * 4 + [table] * 2
    in_specs += [piece] * (3 * pieces)
    args = [gain, wq, wk, wv, wo, cos, sin] + [p for side in sides for p in side]
    aliases = {}
    if prev is not None:
        in_specs.append(pl.BlockSpec(memory_space=pl.ANY))
        aliases = {2 + len(args): 0}
        args.append(prev)
    wide = NEIGHBOUR_COUNT * BLOCK
    spec = pltpu.PrefetchScalarGridSpec(
        num_scalar_prefetch=2,
        grid=(step, blocks),
        in_specs=in_specs,
        out_specs=pl.BlockSpec((1, BLOCK, width), lambda f, b, *_: (f + chunk * step, b, 0)),
        scratch_shapes=[
            pltpu.VMEM((width, width), BF16),
            pltpu.VMEM((width, width), BF16),
            pltpu.VMEM((tokens, width), BF16),
            pltpu.VMEM((3 * tokens, width), BF16),
            pltpu.VMEM((3 * tokens, width), BF16),
            pltpu.VMEM((tokens, width), BF16),
            pltpu.VMEM((wide, width), BF16),
            pltpu.VMEM((wide, width), BF16),
            pltpu.SMEM((1,), F32),
        ],
    )
    return pl.pallas_call(
        functools.partial(space_kernel, scale, pieces, prev is not None),
        grid_spec=spec,
        out_shape=jax.ShapeDtypeStruct((step * chunks, tokens, width), BF16),
        input_output_aliases=aliases,
        compiler_params=pltpu.CompilerParams(vmem_limit_bytes=56 << 20),
        name="space_attention",
    )(ids, pos, *args)


def rotary_tables(tokens, width):
    half = width // HEADS // 2
    freqs = np.power(10000.0, -np.arange(half, dtype=np.float64) / half)
    angle = (np.arange(tokens) % ROT_PERIOD)[:, None] * freqs[None, :]
    cos = np.tile(np.cos(angle).astype(np.float32), (1, HEADS))
    sin = np.tile(np.sin(angle).astype(np.float32), (1, HEADS))
    return jnp.asarray(cos), jnp.asarray(sin)


def body(
    state_tokens,
    gain_time,
    query_time,
    key_time,
    value_time,
    output_time,
    gain_space,
    query_space,
    key_space,
    value_space,
    output_space,
    neighbours,
):
    frames_here, tokens_here, width = state_tokens.shape
    frame_count = lax.axis_size("frame")
    tile_count = lax.axis_size("tile")
    me = lax.axis_index("frame")
    tile = lax.axis_index("tile")
    chunks = FRAME_CHUNKS if frames_here % FRAME_CHUNKS == 0 else 1
    rows = tokens_here // frame_count

    def swap(value, k):
        return lax.ppermute(value, "frame", [(i, i ^ k) for i in range(frame_count)])

    pieces = []
    for k in range(frame_count):
        part = lax.dynamic_slice_in_dim(state_tokens, (me ^ k) * rows, rows, axis=1)
        pieces.append(part if k == 0 else swap(part, k))
    outs = time_stage(
        pieces, chunks, gain_time.reshape(1, width), query_time, key_time, value_time, output_time
    )

    pairs = [(i, i ^ 1) for i in range(tile_count)]
    onward = [(i, (i + 2) % tile_count if i % 2 == 0 else (i - 2) % tile_count) for i in range(tile_count)]
    split = rows % BLOCK == 0
    places = me ^ jnp.arange(frame_count, dtype=jnp.int32)
    sides = []
    for j in range(chunks):
        own = [outs[k * chunks + j] for k in range(frame_count)]
        own = [p if k == 0 else swap(p, k) for k, p in enumerate(own)]
        if not split:
            stacked = jnp.stack(own, axis=1)[:, places]
            own = [stacked.reshape(-1, tokens_here, width)]
        near = [lax.ppermute(p, "tile", pairs) for p in own]
        far = [lax.ppermute(p, "tile", onward) for p in near]
        sides.append((own, near, far))

    blocks = tokens_here // BLOCK
    total = blocks * tile_count
    even = tile % 2 == 0
    offset = (neighbours - (tile - 1) * blocks) % total
    side_of = offset // blocks
    side_at = jnp.where(side_of == 1, 0, jnp.where((side_of == 2) == even, 1, 2))
    inner = offset % blocks
    own_inner = jnp.arange(blocks, dtype=jnp.int32)
    if split:
        per = rows // BLOCK
        inner = ((inner // per) ^ me) * per + inner % per
        own_inner = ((own_inner // per) ^ me) * per + own_inner % per
        pos = (places * rows).astype(jnp.int32)
    else:
        pos = jnp.zeros((1,), jnp.int32)
    present = neighbours >= 0
    ids = jnp.where(present, side_at * blocks + inner, own_inner[:, None])
    ids = jnp.concatenate(
        [ids, present[:, -1:].astype(jnp.int32), own_inner[:, None]], axis=1
    ).reshape(-1)
    cos, sin = rotary_tables(tokens_here, width)
    result = None
    for j in range(chunks):
        result = space_stage(
            sides[j], ids, pos, gain_space.reshape(1, width), query_space, key_space, value_space,
            output_space, cos, sin, result, j, chunks,
        )
    return result


def solution(mesh):
    rows = P("frame", "tile", None)
    return jax.shard_map(
        body,
        mesh=mesh,
        in_specs=(rows,) + (P(),) * 10 + (P("tile", None),),
        out_specs=rows,
        check_vma=False,
    )
```

time: 811 us -> 231 us (0.28); the launches traced: 799 us -> 229 us
  matrix products: 487 us -> 0 us
  local copies, waits for them, and re-layouts: 147 us -> 3.79 us
  Pallas kernels: 0 us -> 119 us
  waiting for transfers between devices: 105 us -> 51.3 us
  starting transfers between devices: 9.38 us -> 53.8 us
  blocking collectives: 29.8 us -> 0 us
  other arithmetic: 14 us -> 0.78 us
    dot_general x41 -> x0, matrix products: 364 us -> none  [the longest x16 198 us: attend_group(): jnp.einsum('fbqk,fbkd->fbqd', weights, gathered_values[..., lower:upper],...]
    sub x17 -> x0, matrix products: 123 us -> none  [the longest x16 108 us: attend_group(): weights = jax.nn.softmax(scores, axis=-1).astype(jnp.bfloat16)]
    pallas_call x0 -> x5, Pallas kernels: none -> 119 us  [the longest x4 100 us: space_stage(): pl.pallas_call(functools.partial(space_kernel, scale, pieces, prev is not...]
    gather x8 -> x0, local copies, waits for them, and re-layouts: 68.4 us -> none  [the longest x4 34.6 us: attend_group(): key_blocks[:, block_ids]]
    ppermute x2 -> x47, starting transfers between devices: 4.59 us -> 53.8 us  [the longest x16 26.3 us: body(): near = [lax.ppermute(p, 'tile', pairs) for p in own]]
    reshape x4 -> x1, local copies, waits for them, and re-layouts: 37.9 us -> 0.62 us  [body(): ids = jnp.concatenate([ids, present[:, -1:].astype(jnp.int32), own_inner[...]
    all_to_all x1 -> x0, blocking collectives: 29.8 us -> none  [body(): lax.all_to_all(split_rows, 'frame', split_axis=1, concat_axis=0, tiled=True)]
    ppermute x2 -> x47, waiting for transfers between devices: 79.1 us -> 51.3 us  [the longest x15 30.7 us: swap(): lax.ppermute(value, 'frame', [(i, i ^ k) for i in range(frame_count)])]
  transfers between devices with their start and end apart: 3 -> 47, of which waited for: 2 -> 20; matrix products, arithmetic and copies ran while one was open for 1% -> 1% of each run, Pallas kernels for 0% -> 33%
where the time goes in v1:
time: 231 us; the launch traced here: 229 us
  Pallas kernels  119 us (52%)
  starting transfers between devices  53.8 us (23%)
  waiting for transfers between devices  51.3 us (22%)
  local copies, waits for them, and re-layouts  3.79 us (2%)
    pallas_call x4, Pallas kernels, space_stage(): pl.pallas_call(functools.partial(space_kernel, scale, pieces, prev is not...  100 us
    ppermute x15, waiting for transfers between devices, swap(): lax.ppermute(value, 'frame', [(i, i ^ k) for i in range(frame_count)])  30.7 us
    ppermute x16, starting transfers between devices, body(): near = [lax.ppermute(p, 'tile', pairs) for p in own]  26.3 us
    pallas_call x1, Pallas kernels, time_stage(): pl.pallas_call(functools.partial(time_kernel, scale, len(pieces), chunks)...  18.7 us
    ppermute x16, starting transfers between devices, body(): far = [lax.ppermute(p, 'tile', onward) for p in near]  16.3 us
    ppermute x16, waiting for transfers between devices, body(): far = [lax.ppermute(p, 'tile', onward) for p in near]  14.9 us
    ppermute x15, starting transfers between devices, swap(): lax.ppermute(value, 'frame', [(i, i ^ k) for i in range(frame_count)])  11.2 us
    ppermute x16, waiting for transfers between devices, body(): near = [lax.ppermute(p, 'tile', pairs) for p in own]  5.72 us
  transfers between devices with their start and end apart: 47, of which 20 were waited for; matrix products, arithmetic and copies ran while one was open for 1% of the time, Pallas kernels for 33%

profile of v1, /device:TPU:0, one launch (start us, length us, event | category | flops | bytes accessed | tf_op | source)
XLA Modules:
  0.0 228.8 jit_solution(5137930279207240390)
XLA Ops:
  0.0 1.7 constant_dynamic-slice_fusion
  2.3 2.6 %collective-permute-start.1 = (bf16[4,256,256]{2,1,0:T(8,128)(2,1)S(1)}, bf16[4,256,256]{2,1,0:T(8,128)(2,1)S(1)}, u32[]{:S(2)}, u32[]{:S(2)}) collective-permute-start(bf16[4,256,256]{2,1,0:T(8,128)(2,1)S(1)} %get-tuple-element.40), channel_id=1, source_target_pairs={{0,16},{8,24},{16,0},{24,8},{1,17},{9,25},{17,1},{25,9},{2,18},{10... | collective-permute-start | bytes 1572872 | tf_op jit(solution)/shard_map/ppermute | solution.py:277
  5.0 12.7 %collective-permute-done.1.refs_2_ = bf16[4,256,256]{2,1,0:T(8,128)(2,1)S(1)} collective-permute-done((bf16[4,256,256]{2,1,0:T(8,128)(2,1)S(1)}, bf16[4,256,256]{2,1,0:T(8,128)(2,1)S(1)}, u32[]{:S(2)}, u32[]{:S(2)}) %collective-permute-start.1) | collective-permute-done | bytes 524320 | tf_op jit(solution)/shard_map/ppermute | solution.py:277
  17.7 10.7 %collective-permute-done.2.refs_3_ = bf16[4,256,256]{2,1,0:T(8,128)(2,1)S(1)} collective-permute-done((bf16[4,256,256]{2,1,0:T(8,128)(2,1)S(1)}, bf16[4,256,256]{2,1,0:T(8,128)(2,1)S(1)}, u32[]{:S(2)}, u32[]{:S(2)}) %collective-permute-start.2) | collective-permute-done | bytes 524320 | tf_op jit(solution)/shard_map/ppermute | solution.py:277
  28.4 18.7 %time_attention.1 = (bf16[1,256,256]{2,1,0:T(8,128)(2,1)S(1)}, bf16[1,256,256]{2,1,0:T(8,128)(2,1)S(1)}, bf16[1,256,256]{2,1,0:T(8,128)(2,1)S(1)}, bf16[1,256,25...) custom-call(f32[1,256]{1,0:T(1,128)S(1)} %bitcast.2, ...), custom_call_target="tpu_custom_call" | custom-call | tf_op jit(solution)/shard_map/time_attention/pallas_call | solution.py:87
  47.4 1.7 collective-permute-start.37
  49.1 1.6 collective-permute-start.39
  51.0 1.5 collective-permute-start.26
  52.5 1.2 collective-permute-done.37.refs_2_
  53.7 2.0 collective-permute-done.38.refs_3_
  55.7 1.5 collective-permute-start.28
  57.8 1.5 collective-permute-start.15
  59.4 2.0 collective-permute-done.27.refs_3_
  61.4 1.5 collective-permute-start.17
  63.4 1.5 collective-permute-start.4
  65.0 2.0 collective-permute-done.16.refs_3_
  67.0 1.5 collective-permute-start.6
  69.1 1.4 collective-permute-start.41
  70.5 1.8 collective-permute-start.42
  72.4 1.5 collective-permute-start.43
  73.9 3.4 %collective-permute-start.29 = (bf16[1,256,256]{2,1,0:T(8,128)(2,1)S(1)}, bf16[1,256,256]{2,1,0:T(8,128)(2,1)S(1)}, u32[]{:S(2)}, u32[]{:S(2)}) collective-permute-start(bf16[1,256,256]{2,1,0:T(8,128)(2,1)S(1)} %collective-permute-done.25.refs_1_), channel_id=1, source_target_pairs={{0,1},{1,0},{2,3},{3,2},{4,5},{5,4},{6,7},{7,6},{8,9},{9,8},{10,11... | collective-permute-start | bytes 393224 | tf_op jit(solution)/shard_map/ppermute | solution.py:298
  77.7 1.3 collective-permute-done.41.refs_6_
  79.0 1.6 collective-permute-start.31
  80.6 1.1 collective-permute-done.42.refs_7_
  82.3 1.7 collective-permute-start.32
  84.0 3.6 %collective-permute-start.18 = (bf16[1,256,256]{2,1,0:T(8,128)(2,1)S(1)}, bf16[1,256,256]{2,1,0:T(8,128)(2,1)S(1)}, u32[]{:S(2)}, u32[]{:S(2)}) collective-permute-start(bf16[1,256,256]{2,1,0:T(8,128)(2,1)S(1)} %collective-permute-done.14.refs_1_), channel_id=1, source_target_pairs={{0,1},{1,0},{2,3},{3,2},{4,5},{5,4},{6,7},{7,6},{8,9},{9,8},{10,11... | collective-permute-start | bytes 393224 | tf_op jit(solution)/shard_map/ppermute | solution.py:298
  88.2 1.5 collective-permute-start.20
  90.1 1.7 collective-permute-start.21
  91.8 3.5 %collective-permute-start.7 = (bf16[1,256,256]{2,1,0:T(8,128)(2,1)S(1)}, bf16[1,256,256]{2,1,0:T(8,128)(2,1)S(1)}, u32[]{:S(2)}, u32[]{:S(2)}) collective-permute-start(bf16[1,256,256]{2,1,0:T(8,128)(2,1)S(1)} %collective-permute-done.3.refs_1_), channel_id=1, source_target_pairs={{0,1},{1,0},{2,3},{3,2},{4,5},{5,4},{6,7},{7,6},{8,9},{9,8},{10,11... | collective-permute-start | bytes 393224 | tf_op jit(solution)/shard_map/ppermute | solution.py:298
  95.7 1.8 collective-permute-start.9
  97.5 1.1 collective-permute-done.20.refs_7_
  98.5 1.7 collective-permute-start.44
  100.2 1.6 collective-permute-start.45
  101.8 1.6 collective-permute-start.46
  104.2 1.7 collective-permute-start.33
  106.7 1.8 collective-permute-start.34
  108.5 1.6 collective-permute-start.35
  110.0 1.6 collective-permute-start.22
  111.6 1.0 collective-permute-done.46.refs_11_
  112.7 2.6 %collective-permute-done.33.refs_9_ = bf16[1,256,256]{2,1,0:T(8,128)(2,1)S(1)} collective-permute-done((bf16[1,256,256]{2,1,0:T(8,128)(2,1)S(1)}, bf16[1,256,256]{2,1,0:T(8,128)(2,1)S(1)}, u32[]{:S(2)}, u32[]{:S(2)}) %collective-permute-start.33) | collective-permute-done | bytes 131104 | tf_op jit(solution)/shard_map/ppermute | solution.py:299
  115.3 2.8 %collective-permute-done.34.refs_10_ = bf16[1,256,256]{2,1,0:T(8,128)(2,1)S(1)} collective-permute-done((bf16[1,256,256]{2,1,0:T(8,128)(2,1)S(1)}, bf16[1,256,256]{2,1,0:T(8,128)(2,1)S(1)}, u32[]{:S(2)}, u32[]{:S(2)}) %collective-permute-start.34) | collective-permute-done | bytes 131104 | tf_op jit(solution)/shard_map/ppermute | solution.py:299
  118.2 2.8 %collective-permute-done.35.refs_11_ = bf16[1,256,256]{2,1,0:T(8,128)(2,1)S(1)} collective-permute-done((bf16[1,256,256]{2,1,0:T(8,128)(2,1)S(1)}, bf16[1,256,256]{2,1,0:T(8,128)(2,1)S(1)}, u32[]{:S(2)}, u32[]{:S(2)}) %collective-permute-start.35) | collective-permute-done | bytes 131104 | tf_op jit(solution)/shard_map/ppermute | solution.py:299
  121.0 2.8 %collective-permute-done.22.refs_9_ = bf16[1,256,256]{2,1,0:T(8,128)(2,1)S(1)} collective-permute-done((bf16[1,256,256]{2,1,0:T(8,128)(2,1)S(1)}, bf16[1,256,256]{2,1,0:T(8,128)(2,1)S(1)}, u32[]{:S(2)}, u32[]{:S(2)}) %collective-permute-start.22) | collective-permute-done | bytes 131104 | tf_op jit(solution)/shard_map/ppermute | solution.py:299
  123.8 2.8 %collective-permute-done.23.refs_10_ = bf16[1,256,256]{2,1,0:T(8,128)(2,1)S(1)} collective-permute-done((bf16[1,256,256]{2,1,0:T(8,128)(2,1)S(1)}, bf16[1,256,256]{2,1,0:T(8,128)(2,1)S(1)}, u32[]{:S(2)}, u32[]{:S(2)}) %collective-permute-start.23) | collective-permute-done | bytes 131104 | tf_op jit(solution)/shard_map/ppermute | solution.py:299
  128.5 24.8 %space_attention.4.refs_12_ = bf16[4,1024,256]{2,1,0:T(8,128)(2,1)} custom-call(s32[88]{0:T(128)} %reshape.71.ids, s32[4]{0:T(128)} %xor_multiply_fusion.pos, f32[1,256]{1,0:T(1,128)} %bitcast.3, bf16[256,256]{1,0:T(8,128)(2,1)} %wq_ref.9, bf16[256,256]{1,0:T(8,128)(2,1)} %wk_ref.9, bf16[256,256]{1,0:T(8,128)(2,1)} %wv_ref.9, bf16[256,256]{1,0:T(8,128)(2,1)} %wo_ref.9, ...), custom_call_target="tpu_custom_call" | custom-call | tf_op jit(solution)/shard_map/space_attention/pallas_call | solution.py:235
  153.5 25.0 %space_attention.5.refs_12_ = bf16[4,1024,256]{2,1,0:T(8,128)(2,1)} custom-call(s32[88]{0:T(128)} %reshape.71.ids, s32[4]{0:T(128)} %xor_multiply_fusion.pos, f32[1,256]{1,0:T(1,128)} %bitcast.4, bf16[256,256]{1,0:T(8,128)(2,1)} %wq_ref.9, bf16[256,256]{1,0:T(8,128)(2,1)} %wk_ref.9, bf16[256,256]{1,0:T(8,128)(2,1)} %wv_ref.9, ...), custom_call_target="tpu_custom_call", output_to_operand_aliasing={{}: (21, {})} | custom-call | tf_op jit(solution)/shard_map/space_attention/pallas_call | solution.py:235
  178.5 25.1 %space_attention.6.refs_12_ = bf16[4,1024,256]{2,1,0:T(8,128)(2,1)} custom-call(s32[88]{0:T(128)} %reshape.71.ids, s32[4]{0:T(128)} %xor_multiply_fusion.pos, f32[1,256]{1,0:T(1,128)} %bitcast.5, bf16[256,256]{1,0:T(8,128)(2,1)} %wq_ref.9, bf16[256,256]{1,0:T(8,128)(2,1)} %wk_ref.9, bf16[256,256]{1,0:T(8,128)(2,1)} %wv_ref.9, ...), custom_call_target="tpu_custom_call", output_to_operand_aliasing={{}: (21, {})} | custom-call | tf_op jit(solution)/shard_map/space_attention/pallas_call | solution.py:235
  203.7 25.1 %space_attention.7 = bf16[4,1024,256]{2,1,0:T(8,128)(2,1)} custom-call(s32[88]{0:T(128)} %reshape.71.ids, s32[4]{0:T(128)} %xor_multiply_fusion.pos, f32[1,256]{1,0:T(1,128)} %bitcast.6, bf16[256,256]{1,0:T(8,128)(2,1)} %wq_ref.9, bf16[256,256]{1,0:T(8,128)(2,1)} %wk_ref.9, bf16[256,256]{1,0:T(8,128)(2,1)} %wv_ref.9, ...), custom_call_target="tpu_custom_call", output_to_operand_aliasing={{}: (21, {})} | custom-call | tf_op jit(solution)/shard_map/space_attention/pallas_call | solution.py:235
  (150 shorter events, 9.2 us)
Async XLA Ops:
  1.8 3.2 %collective-permute-start = (bf16[4,256,256]{2,1,0:T(8,128)(2,1)S(1)}, bf16[4,256,256]{2,1,0:T(8,128)(2,1)S(1)}, u32[]{:S(2)}, u32[]{:S(2)}) collective-permute-start(bf16[4,256,256]{2,1,0:T(8,128)(2,1)S(1)} %get-tuple-element.38), channel_id=1, source_target_pairs={{0,8},{8,0},{16,24},{24,16},{1,9},{9,1},{17,25},{25,17},{2,10},{10... | collective-permute-start | bytes 1572872 | tf_op jit(solution)/shard_map/ppermute | solution.py:277
  2.3 15.3 %collective-permute-start.1 = (bf16[4,256,256]{2,1,0:T(8,128)(2,1)S(1)}, bf16[4,256,256]{2,1,0:T(8,128)(2,1)S(1)}, u32[]{:S(2)}, u32[]{:S(2)}) collective-permute-start(bf16[4,256,256]{2,1,0:T(8,128)(2,1)S(1)} %get-tuple-element.40), channel_id=1, source_target_pairs={{0,16},{8,24},{16,0},{24,8},{1,17},{9,25},{17,1},{25,9},{2,18},{10... | collective-permute-start | bytes 1572872 | tf_op jit(solution)/shard_map/ppermute | solution.py:277
  4.9 23.5 %collective-permute-start.2 = (bf16[4,256,256]{2,1,0:T(8,128)(2,1)S(1)}, bf16[4,256,256]{2,1,0:T(8,128)(2,1)S(1)}, u32[]{:S(2)}, u32[]{:S(2)}) collective-permute-start(bf16[4,256,256]{2,1,0:T(8,128)(2,1)S(1)} %get-tuple-element.37), channel_id=1, source_target_pairs={{0,24},{8,16},{16,8},{24,0},{1,25},{9,17},{17,9},{25,1},{2,26},{10... | collective-permute-start | bytes 1572872 | tf_op jit(solution)/shard_map/ppermute | solution.py:277
  47.1 106.1 %copy-start = (bf16[1,256,256]{2,1,0:T(8,128)(2,1)}, bf16[1,256,256]{2,1,0:T(8,128)(2,1)S(1)}, u32[]{:S(2)}) copy-start(bf16[1,256,256]{2,1,0:T(8,128)(2,1)S(1)} %get-tuple-element.21.refs_0_) | copy-start | bytes 393220
  47.2 3.8 %collective-permute-start.36 = (bf16[1,256,256]{2,1,0:T(8,128)(2,1)S(1)}, bf16[1,256,256]{2,1,0:T(8,128)(2,1)S(1)}, u32[]{:S(2)}, u32[]{:S(2)}) collective-permute-start(bf16[1,256,256]{2,1,0:T(8,128)(2,1)S(1)} %get-tuple-element.34), channel_id=1, source_target_pairs={{0,8},{8,0},{16,24},{24,16},{1,9},{9,1},{17,25},{25,17},{2,10},{10... | collective-permute-start | bytes 393224 | tf_op jit(solution)/shard_map/ppermute | solution.py:277
  47.4 6.3 %collective-permute-start.37 = (bf16[1,256,256]{2,1,0:T(8,128)(2,1)S(1)}, bf16[1,256,256]{2,1,0:T(8,128)(2,1)S(1)}, u32[]{:S(2)}, u32[]{:S(2)}) collective-permute-start(bf16[1,256,256]{2,1,0:T(8,128)(2,1)S(1)} %get-tuple-element.35), channel_id=1, source_target_pairs={{0,16},{8,24},{16,0},{24,8},{1,17},{9,25},{17,1},{25,9},{2,18},{10... | collective-permute-start | bytes 393224 | tf_op jit(solution)/shard_map/ppermute | solution.py:277
  49.1 6.7 %collective-permute-start.38 = (bf16[1,256,256]{2,1,0:T(8,128)(2,1)S(1)}, bf16[1,256,256]{2,1,0:T(8,128)(2,1)S(1)}, u32[]{:S(2)}, u32[]{:S(2)}) collective-permute-start(bf16[1,256,256]{2,1,0:T(8,128)(2,1)S(1)} %get-tuple-element.36), channel_id=1, source_target_pairs={{0,24},{8,16},{16,8},{24,0},{1,25},{9,17},{17,9},{25,1},{2,26},{10... | collective-permute-start | bytes 393224 | tf_op jit(solution)/shard_map/ppermute | solution.py:277
  49.1 8.1 %collective-permute-start.39 = (bf16[1,256,256]{2,1,0:T(8,128)(2,1)S(1)}, bf16[1,256,256]{2,1,0:T(8,128)(2,1)S(1)}, u32[]{:S(2)}, u32[]{:S(2)}) collective-permute-start(bf16[1,256,256]{2,1,0:T(8,128)(2,1)S(1)} %get-tuple-element.33.refs_0_), channel_id=1, source_target_pairs={{0,1},{1,0},{2,3},{3,2},{4,5},{5,4},{6,7},{7,6},{8,9},{9,8},{10,11... | collective-permute-start | bytes 393224 | tf_op jit(solution)/shard_map/ppermute | solution.py:298
  50.7 7.1 %collective-permute-start.25 = (bf16[1,256,256]{2,1,0:T(8,128)(2,1)S(1)}, bf16[1,256,256]{2,1,0:T(8,128)(2,1)S(1)}, u32[]{:S(2)}, u32[]{:S(2)}) collective-permute-start(bf16[1,256,256]{2,1,0:T(8,128)(2,1)S(1)} %get-tuple-element.30), channel_id=1, source_target_pairs={{0,8},{8,0},{16,24},{24,16},{1,9},{9,1},{17,25},{25,17},{2,10},{10... | collective-permute-start | bytes 393224 | tf_op jit(solution)/shard_map/ppermute | solution.py:277
  51.0 8.3 %collective-permute-start.26 = (bf16[1,256,256]{2,1,0:T(8,128)(2,1)S(1)}, bf16[1,256,256]{2,1,0:T(8,128)(2,1)S(1)}, u32[]{:S(2)}, u32[]{:S(2)}) collective-permute-start(bf16[1,256,256]{2,1,0:T(8,128)(2,1)S(1)} %get-tuple-element.31), channel_id=1, source_target_pairs={{0,16},{8,24},{16,0},{24,8},{1,17},{9,25},{17,1},{25,9},{2,18},{10... | collective-permute-start | bytes 393224 | tf_op jit(solution)/shard_map/ppermute | solution.py:277
  53.7 7.7 %collective-permute-start.27 = (bf16[1,256,256]{2,1,0:T(8,128)(2,1)S(1)}, bf16[1,256,256]{2,1,0:T(8,128)(2,1)S(1)}, u32[]{:S(2)}, u32[]{:S(2)}) collective-permute-start(bf16[1,256,256]{2,1,0:T(8,128)(2,1)S(1)} %get-tuple-element.32), channel_id=1, source_target_pairs={{0,24},{8,16},{16,8},{24,0},{1,25},{9,17},{17,9},{25,1},{2,26},{10... | collective-permute-start | bytes 393224 | tf_op jit(solution)/shard_map/ppermute | solution.py:277
  55.7 7.1 %collective-permute-start.28 = (bf16[1,256,256]{2,1,0:T(8,128)(2,1)S(1)}, bf16[1,256,256]{2,1,0:T(8,128)(2,1)S(1)}, u32[]{:S(2)}, u32[]{:S(2)}) collective-permute-start(bf16[1,256,256]{2,1,0:T(8,128)(2,1)S(1)} %get-tuple-element.29.refs_0_), channel_id=1, source_target_pairs={{0,1},{1,0},{2,3},{3,2},{4,5},{5,4},{6,7},{7,6},{8,9},{9,8},{10,11... | collective-permute-start | bytes 393224 | tf_op jit(solution)/shard_map/ppermute | solution.py:298
  57.3 6.2 %collective-permute-start.14 = (bf16[1,256,256]{2,1,0:T(8,128)(2,1)S(1)}, bf16[1,256,256]{2,1,0:T(8,128)(2,1)S(1)}, u32[]{:S(2)}, u32[]{:S(2)}) collective-permute-start(bf16[1,256,256]{2,1,0:T(8,128)(2,1)S(1)} %get-tuple-element.26), channel_id=1, source_target_pairs={{0,8},{8,0},{16,24},{24,16},{1,9},{9,1},{17,25},{25,17},{2,10},{10... | collective-permute-start | bytes 393224 | tf_op jit(solution)/shard_map/ppermute | solution.py:277
  57.8 7.1 %collective-permute-start.15 = (bf16[1,256,256]{2,1,0:T(8,128)(2,1)S(1)}, bf16[1,256,256]{2,1,0:T(8,128)(2,1)S(1)}, u32[]{:S(2)}, u32[]{:S(2)}) collective-permute-start(bf16[1,256,256]{2,1,0:T(8,128)(2,1)S(1)} %get-tuple-element.27), channel_id=1, source_target_pairs={{0,16},{8,24},{16,0},{24,8},{1,17},{9,25},{17,1},{25,9},{2,18},{10... | collective-permute-start | bytes 393224 | tf_op jit(solution)/shard_map/ppermute | solution.py:277
  59.3 7.7 %collective-permute-start.16 = (bf16[1,256,256]{2,1,0:T(8,128)(2,1)S(1)}, bf16[1,256,256]{2,1,0:T(8,128)(2,1)S(1)}, u32[]{:S(2)}, u32[]{:S(2)}) collective-permute-start(bf16[1,256,256]{2,1,0:T(8,128)(2,1)S(1)} %get-tuple-element.28), channel_id=1, source_target_pairs={{0,24},{8,16},{16,8},{24,0},{1,25},{9,17},{17,9},{25,1},{2,26},{10... | collective-permute-start | bytes 393224 | tf_op jit(solution)/shard_map/ppermute | solution.py:277
  61.4 7.1 %collective-permute-start.17 = (bf16[1,256,256]{2,1,0:T(8,128)(2,1)S(1)}, bf16[1,256,256]{2,1,0:T(8,128)(2,1)S(1)}, u32[]{:S(2)}, u32[]{:S(2)}) collective-permute-start(bf16[1,256,256]{2,1,0:T(8,128)(2,1)S(1)} %get-tuple-element.25.refs_0_), channel_id=1, source_target_pairs={{0,1},{1,0},{2,3},{3,2},{4,5},{5,4},{6,7},{7,6},{8,9},{9,8},{10,11... | collective-permute-start | bytes 393224 | tf_op jit(solution)/shard_map/ppermute | solution.py:298
  62.9 6.2 %collective-permute-start.3 = (bf16[1,256,256]{2,1,0:T(8,128)(2,1)S(1)}, bf16[1,256,256]{2,1,0:T(8,128)(2,1)S(1)}, u32[]{:S(2)}, u32[]{:S(2)}) collective-permute-start(bf16[1,256,256]{2,1,0:T(8,128)(2,1)S(1)} %get-tuple-element.22), channel_id=1, source_target_pairs={{0,8},{8,0},{16,24},{24,16},{1,9},{9,1},{17,25},{25,17},{2,10},{10... | collective-permute-start | bytes 393224 | tf_op jit(solution)/shard_map/ppermute | solution.py:277
  63.4 7.1 %collective-permute-start.4 = (bf16[1,256,256]{2,1,0:T(8,128)(2,1)S(1)}, bf16[1,256,256]{2,1,0:T(8,128)(2,1)S(1)}, u32[]{:S(2)}, u32[]{:S(2)}) collective-permute-start(bf16[1,256,256]{2,1,0:T(8,128)(2,1)S(1)} %get-tuple-element.23), channel_id=1, source_target_pairs={{0,16},{8,24},{16,0},{24,8},{1,17},{9,25},{17,1},{25,9},{2,18},{10... | collective-permute-start | bytes 393224 | tf_op jit(solution)/shard_map/ppermute | solution.py:277
  64.9 7.5 %collective-permute-start.5 = (bf16[1,256,256]{2,1,0:T(8,128)(2,1)S(1)}, bf16[1,256,256]{2,1,0:T(8,128)(2,1)S(1)}, u32[]{:S(2)}, u32[]{:S(2)}) collective-permute-start(bf16[1,256,256]{2,1,0:T(8,128)(2,1)S(1)} %get-tuple-element.24), channel_id=1, source_target_pairs={{0,24},{8,16},{16,8},{24,0},{1,25},{9,17},{17,9},{25,1},{2,26},{10... | collective-permute-start | bytes 393224 | tf_op jit(solution)/shard_map/ppermute | solution.py:277
  67.0 6.9 %collective-permute-start.6 = (bf16[1,256,256]{2,1,0:T(8,128)(2,1)S(1)}, bf16[1,256,256]{2,1,0:T(8,128)(2,1)S(1)}, u32[]{:S(2)}, u32[]{:S(2)}) collective-permute-start(bf16[1,256,256]{2,1,0:T(8,128)(2,1)S(1)} %get-tuple-element.21.refs_0_), channel_id=1, source_target_pairs={{0,1},{1,0},{2,3},{3,2},{4,5},{5,4},{6,7},{7,6},{8,9},{9,8},{10,11... | collective-permute-start | bytes 393224 | tf_op jit(solution)/shard_map/ppermute | solution.py:298
  68.5 8.8 %collective-permute-start.40 = (bf16[1,256,256]{2,1,0:T(8,128)(2,1)S(1)}, bf16[1,256,256]{2,1,0:T(8,128)(2,1)S(1)}, u32[]{:S(2)}, u32[]{:S(2)}) collective-permute-start(bf16[1,256,256]{2,1,0:T(8,128)(2,1)S(1)} %collective-permute-done.36.refs_1_), channel_id=1, source_target_pairs={{0,1},{1,0},{2,3},{3,2},{4,5},{5,4},{6,7},{7,6},{8,9},{9,8},{10,11... | collective-permute-start | bytes 393224 | tf_op jit(solution)/shard_map/ppermute | solution.py:298
  69.1 9.9 %collective-permute-start.41 = (bf16[1,256,256]{2,1,0:T(8,128)(2,1)S(1)}, bf16[1,256,256]{2,1,0:T(8,128)(2,1)}, u32[]{:S(2)}, u32[]{:S(2)}) collective-permute-start(bf16[1,256,256]{2,1,0:T(8,128)(2,1)S(1)} %collective-permute-done.37.refs_2_), channel_id=1, source_target_pairs={{0,1},{1,0},{2,3},{3,2},{4,5},{5,4},{6,7},{7,6},{8,9},{9,8},{10,11... | collective-permute-start | bytes 393224 | tf_op jit(solution)/shard_map/ppermute | solution.py:298
  70.5 11.1 %collective-permute-start.42 = (bf16[1,256,256]{2,1,0:T(8,128)(2,1)S(1)}, bf16[1,256,256]{2,1,0:T(8,128)(2,1)S(1)}, u32[]{:S(2)}, u32[]{:S(2)}) collective-permute-start(bf16[1,256,256]{2,1,0:T(8,128)(2,1)S(1)} %collective-permute-done.38.refs_3_), channel_id=1, source_target_pairs={{0,1},{1,0},{2,3},{3,2},{4,5},{5,4},{6,7},{7,6},{8,9},{9,8},{10,11... | collective-permute-start | bytes 393224 | tf_op jit(solution)/shard_map/ppermute | solution.py:298
  72.4 11.7 %collective-permute-start.43 = (bf16[1,256,256]{2,1,0:T(8,128)(2,1)S(1)}, bf16[1,256,256]{2,1,0:T(8,128)(2,1)S(1)}, u32[]{:S(2)}, u32[]{:S(2)}) collective-permute-start(bf16[1,256,256]{2,1,0:T(8,128)(2,1)S(1)} %collective-permute-done.39.refs_4_), channel_id=1, source_target_pairs={{0,2},{1,7},{2,4},{3,1},{4,6},{5,3},{6,0},{7,5},{8,10},{9,15},{10,... | collective-permute-start | bytes 393224 | tf_op jit(solution)/shard_map/ppermute | solution.py:299
  73.9 13.8 %collective-permute-start.29 = (bf16[1,256,256]{2,1,0:T(8,128)(2,1)S(1)}, bf16[1,256,256]{2,1,0:T(8,128)(2,1)S(1)}, u32[]{:S(2)}, u32[]{:S(2)}) collective-permute-start(bf16[1,256,256]{2,1,0:T(8,128)(2,1)S(1)} %collective-permute-done.25.refs_1_), channel_id=1, source_target_pairs={{0,1},{1,0},{2,3},{3,2},{4,5},{5,4},{6,7},{7,6},{8,9},{9,8},{10,11... | collective-permute-start | bytes 393224 | tf_op jit(solution)/shard_map/ppermute | solution.py:298
  77.3 10.9 %collective-permute-start.30 = (bf16[1,256,256]{2,1,0:T(8,128)(2,1)S(1)}, bf16[1,256,256]{2,1,0:T(8,128)(2,1)S(1)}, u32[]{:S(2)}, u32[]{:S(2)}) collective-permute-start(bf16[1,256,256]{2,1,0:T(8,128)(2,1)S(1)} %collective-permute-done.26.refs_2_), channel_id=1, source_target_pairs={{0,1},{1,0},{2,3},{3,2},{4,5},{5,4},{6,7},{7,6},{8,9},{9,8},{10,11... | collective-permute-start | bytes 393224 | tf_op jit(solution)/shard_map/ppermute | solution.py:298
  79.0 11.1 %collective-permute-start.31 = (bf16[1,256,256]{2,1,0:T(8,128)(2,1)S(1)}, bf16[1,256,256]{2,1,0:T(8,128)(2,1)S(1)}, u32[]{:S(2)}, u32[]{:S(2)}) collective-permute-start(bf16[1,256,256]{2,1,0:T(8,128)(2,1)S(1)} %collective-permute-done.27.refs_3_), channel_id=1, source_target_pairs={{0,1},{1,0},{2,3},{3,2},{4,5},{5,4},{6,7},{7,6},{8,9},{9,8},{10,11... | collective-permute-start | bytes 393224 | tf_op jit(solution)/shard_map/ppermute | solution.py:298
  82.3 9.4 %collective-permute-start.32 = (bf16[1,256,256]{2,1,0:T(8,128)(2,1)S(1)}, bf16[1,256,256]{2,1,0:T(8,128)(2,1)S(1)}, u32[]{:S(2)}, u32[]{:S(2)}) collective-permute-start(bf16[1,256,256]{2,1,0:T(8,128)(2,1)S(1)} %collective-permute-done.28.refs_4_), channel_id=1, source_target_pairs={{0,2},{1,7},{2,4},{3,1},{4,6},{5,3},{6,0},{7,5},{8,10},{9,15},{10,... | collective-permute-start | bytes 393224 | tf_op jit(solution)/shard_map/ppermute | solution.py:299
  84.0 11.4 %collective-permute-start.18 = (bf16[1,256,256]{2,1,0:T(8,128)(2,1)S(1)}, bf16[1,256,256]{2,1,0:T(8,128)(2,1)S(1)}, u32[]{:S(2)}, u32[]{:S(2)}) collective-permute-start(bf16[1,256,256]{2,1,0:T(8,128)(2,1)S(1)} %collective-permute-done.14.refs_1_), channel_id=1, source_target_pairs={{0,1},{1,0},{2,3},{3,2},{4,5},{5,4},{6,7},{7,6},{8,9},{9,8},{10,11... | collective-permute-start | bytes 393224 | tf_op jit(solution)/shard_map/ppermute | solution.py:298
  87.7 8.1 %collective-permute-start.19 = (bf16[1,256,256]{2,1,0:T(8,128)(2,1)S(1)}, bf16[1,256,256]{2,1,0:T(8,128)(2,1)S(1)}, u32[]{:S(2)}, u32[]{:S(2)}) collective-permute-start(bf16[1,256,256]{2,1,0:T(8,128)(2,1)S(1)} %collective-permute-done.15.refs_2_), channel_id=1, source_target_pairs={{0,1},{1,0},{2,3},{3,2},{4,5},{5,4},{6,7},{7,6},{8,9},{9,8},{10,11... | collective-permute-start | bytes 393224 | tf_op jit(solution)/shard_map/ppermute | solution.py:298
  88.2 10.3 %collective-permute-start.20 = (bf16[1,256,256]{2,1,0:T(8,128)(2,1)S(1)}, bf16[1,256,256]{2,1,0:T(8,128)(2,1)S(1)}, u32[]{:S(2)}, u32[]{:S(2)}) collective-permute-start(bf16[1,256,256]{2,1,0:T(8,128)(2,1)S(1)} %collective-permute-done.16.refs_3_), channel_id=1, source_target_pairs={{0,1},{1,0},{2,3},{3,2},{4,5},{5,4},{6,7},{7,6},{8,9},{9,8},{10,11... | collective-permute-start | bytes 393224 | tf_op jit(solution)/shard_map/ppermute | solution.py:298
  90.1 10.1 %collective-permute-start.21 = (bf16[1,256,256]{2,1,0:T(8,128)(2,1)S(1)}, bf16[1,256,256]{2,1,0:T(8,128)(2,1)S(1)}, u32[]{:S(2)}, u32[]{:S(2)}) collective-permute-start(bf16[1,256,256]{2,1,0:T(8,128)(2,1)S(1)} %collective-permute-done.17.refs_4_), channel_id=1, source_target_pairs={{0,2},{1,7},{2,4},{3,1},{4,6},{5,3},{6,0},{7,5},{8,10},{9,15},{10,... | collective-permute-start | bytes 393224 | tf_op jit(solution)/shard_map/ppermute | solution.py:299
  91.8 10.0 %collective-permute-start.7 = (bf16[1,256,256]{2,1,0:T(8,128)(2,1)S(1)}, bf16[1,256,256]{2,1,0:T(8,128)(2,1)S(1)}, u32[]{:S(2)}, u32[]{:S(2)}) collective-permute-start(bf16[1,256,256]{2,1,0:T(8,128)(2,1)S(1)} %collective-permute-done.3.refs_1_), channel_id=1, source_target_pairs={{0,1},{1,0},{2,3},{3,2},{4,5},{5,4},{6,7},{7,6},{8,9},{9,8},{10,11... | collective-permute-start | bytes 393224 | tf_op jit(solution)/shard_map/ppermute | solution.py:298
  95.4 8.7 %collective-permute-start.8 = (bf16[1,256,256]{2,1,0:T(8,128)(2,1)S(1)}, bf16[1,256,256]{2,1,0:T(8,128)(2,1)S(1)}, u32[]{:S(2)}, u32[]{:S(2)}) collective-permute-start(bf16[1,256,256]{2,1,0:T(8,128)(2,1)S(1)} %collective-permute-done.4.refs_2_), channel_id=1, source_target_pairs={{0,1},{1,0},{2,3},{3,2},{4,5},{5,4},{6,7},{7,6},{8,9},{9,8},{10,11... | collective-permute-start | bytes 393224 | tf_op jit(solution)/shard_map/ppermute | solution.py:298
  95.7 10.9 %collective-permute-start.9 = (bf16[1,256,256]{2,1,0:T(8,128)(2,1)S(1)}, bf16[1,256,256]{2,1,0:T(8,128)(2,1)S(1)}, u32[]{:S(2)}, u32[]{:S(2)}) collective-permute-start(bf16[1,256,256]{2,1,0:T(8,128)(2,1)S(1)} %collective-permute-done.5.refs_3_), channel_id=1, source_target_pairs={{0,1},{1,0},{2,3},{3,2},{4,5},{5,4},{6,7},{7,6},{8,9},{9,8},{10,11... | collective-permute-start | bytes 393224 | tf_op jit(solution)/shard_map/ppermute | solution.py:298
  98.5 9.9 %collective-permute-start.44 = (bf16[1,256,256]{2,1,0:T(8,128)(2,1)}, bf16[1,256,256]{2,1,0:T(8,128)(2,1)}, u32[]{:S(2)}, u32[]{:S(2)}) collective-permute-start(bf16[1,256,256]{2,1,0:T(8,128)(2,1)} %copy-done.41), channel_id=1, source_target_pairs={{0,2},{1,7},{2,4},{3,1},{4,6},{5,3},{6,0},{7,5},{8,10},{9,15},{10,... | collective-permute-start | bytes 393224 | tf_op jit(solution)/shard_map/ppermute | solution.py:299
  100.2 9.8 %collective-permute-start.45 = (bf16[1,256,256]{2,1,0:T(8,128)(2,1)}, bf16[1,256,256]{2,1,0:T(8,128)(2,1)}, u32[]{:S(2)}, u32[]{:S(2)}) collective-permute-start(bf16[1,256,256]{2,1,0:T(8,128)(2,1)} %collective-permute-done.41.refs_6_), channel_id=1, source_target_pairs={{0,2},{1,7},{2,4},{3,1},{4,6},{5,3},{6,0},{7,5},{8,10},{9,15},{10,... | collective-permute-start | bytes 393224 | tf_op jit(solution)/shard_map/ppermute | solution.py:299
  101.8 10.8 %collective-permute-start.46 = (bf16[1,256,256]{2,1,0:T(8,128)(2,1)}, bf16[1,256,256]{2,1,0:T(8,128)(2,1)}, u32[]{:S(2)}, u32[]{:S(2)}) collective-permute-start(bf16[1,256,256]{2,1,0:T(8,128)(2,1)} %copy-done.42), channel_id=1, source_target_pairs={{0,2},{1,7},{2,4},{3,1},{4,6},{5,3},{6,0},{7,5},{8,10},{9,15},{10,... | collective-permute-start | bytes 393224 | tf_op jit(solution)/shard_map/ppermute | solution.py:299
  104.2 11.2 %collective-permute-start.33 = (bf16[1,256,256]{2,1,0:T(8,128)(2,1)S(1)}, bf16[1,256,256]{2,1,0:T(8,128)(2,1)S(1)}, u32[]{:S(2)}, u32[]{:S(2)}) collective-permute-start(bf16[1,256,256]{2,1,0:T(8,128)(2,1)S(1)} %collective-permute-done.29.refs_5_), channel_id=1, source_target_pairs={{0,2},{1,7},{2,4},{3,1},{4,6},{5,3},{6,0},{7,5},{8,10},{9,15},{10,... | collective-permute-start | bytes 393224 | tf_op jit(solution)/shard_map/ppermute | solution.py:299
  106.7 11.5 %collective-permute-start.34 = (bf16[1,256,256]{2,1,0:T(8,128)(2,1)S(1)}, bf16[1,256,256]{2,1,0:T(8,128)(2,1)S(1)}, u32[]{:S(2)}, u32[]{:S(2)}) collective-permute-start(bf16[1,256,256]{2,1,0:T(8,128)(2,1)S(1)} %collective-permute-done.30.refs_6_), channel_id=1, source_target_pairs={{0,2},{1,7},{2,4},{3,1},{4,6},{5,3},{6,0},{7,5},{8,10},{9,15},{10,... | collective-permute-start | bytes 393224 | tf_op jit(solution)/shard_map/ppermute | solution.py:299
  108.5 12.5 %collective-permute-start.35 = (bf16[1,256,256]{2,1,0:T(8,128)(2,1)S(1)}, bf16[1,256,256]{2,1,0:T(8,128)(2,1)S(1)}, u32[]{:S(2)}, u32[]{:S(2)}) collective-permute-start(bf16[1,256,256]{2,1,0:T(8,128)(2,1)S(1)} %collective-permute-done.31.refs_7_), channel_id=1, source_target_pairs={{0,2},{1,7},{2,4},{3,1},{4,6},{5,3},{6,0},{7,5},{8,10},{9,15},{10,... | collective-permute-start | bytes 393224 | tf_op jit(solution)/shard_map/ppermute | solution.py:299
  110.0 13.7 %collective-permute-start.22 = (bf16[1,256,256]{2,1,0:T(8,128)(2,1)S(1)}, bf16[1,256,256]{2,1,0:T(8,128)(2,1)S(1)}, u32[]{:S(2)}, u32[]{:S(2)}) collective-permute-start(bf16[1,256,256]{2,1,0:T(8,128)(2,1)S(1)} %collective-permute-done.18.refs_5_), channel_id=1, source_target_pairs={{0,2},{1,7},{2,4},{3,1},{4,6},{5,3},{6,0},{7,5},{8,10},{9,15},{10,... | collective-permute-start | bytes 393224 | tf_op jit(solution)/shard_map/ppermute | solution.py:299
  112.6 13.9 %collective-permute-start.23 = (bf16[1,256,256]{2,1,0:T(8,128)(2,1)S(1)}, bf16[1,256,256]{2,1,0:T(8,128)(2,1)S(1)}, u32[]{:S(2)}, u32[]{:S(2)}) collective-permute-start(bf16[1,256,256]{2,1,0:T(8,128)(2,1)S(1)} %collective-permute-done.19.refs_6_), channel_id=1, source_target_pairs={{0,2},{1,7},{2,4},{3,1},{4,6},{5,3},{6,0},{7,5},{8,10},{9,15},{10,... | collective-permute-start | bytes 393224 | tf_op jit(solution)/shard_map/ppermute | solution.py:299
  115.3 88.3 %collective-permute-start.10 = (bf16[1,256,256]{2,1,0:T(8,128)(2,1)S(1)}, bf16[1,256,256]{2,1,0:T(8,128)(2,1)}, u32[]{:S(2)}, u32[]{:S(2)}) collective-permute-start(bf16[1,256,256]{2,1,0:T(8,128)(2,1)S(1)} %collective-permute-done.6.refs_4_), channel_id=1, source_target_pairs={{0,2},{1,7},{2,4},{3,1},{4,6},{5,3},{6,0},{7,5},{8,10},{9,15},{10,... | collective-permute-start | bytes 393224 | tf_op jit(solution)/shard_map/ppermute | solution.py:299
  118.1 60.4 %collective-permute-start.24 = (bf16[1,256,256]{2,1,0:T(8,128)(2,1)S(1)}, bf16[1,256,256]{2,1,0:T(8,128)(2,1)}, u32[]{:S(2)}, u32[]{:S(2)}) collective-permute-start(bf16[1,256,256]{2,1,0:T(8,128)(2,1)S(1)} %collective-permute-done.20.refs_7_), channel_id=1, source_target_pairs={{0,2},{1,7},{2,4},{3,1},{4,6},{5,3},{6,0},{7,5},{8,10},{9,15},{10,... | collective-permute-start | bytes 393224 | tf_op jit(solution)/shard_map/ppermute | solution.py:299
  121.0 82.7 %collective-permute-start.11 = (bf16[1,256,256]{2,1,0:T(8,128)(2,1)S(1)}, bf16[1,256,256]{2,1,0:T(8,128)(2,1)}, u32[]{:S(2)}, u32[]{:S(2)}) collective-permute-start(bf16[1,256,256]{2,1,0:T(8,128)(2,1)S(1)} %collective-permute-done.7.refs_5_), channel_id=1, source_target_pairs={{0,2},{1,7},{2,4},{3,1},{4,6},{5,3},{6,0},{7,5},{8,10},{9,15},{10,... | collective-permute-start | bytes 393224 | tf_op jit(solution)/shard_map/ppermute | solution.py:299
  123.8 79.9 %collective-permute-start.12 = (bf16[1,256,256]{2,1,0:T(8,128)(2,1)S(1)}, bf16[1,256,256]{2,1,0:T(8,128)(2,1)}, u32[]{:S(2)}, u32[]{:S(2)}) collective-permute-start(bf16[1,256,256]{2,1,0:T(8,128)(2,1)S(1)} %collective-permute-done.8.refs_6_), channel_id=1, source_target_pairs={{0,2},{1,7},{2,4},{3,1},{4,6},{5,3},{6,0},{7,5},{8,10},{9,15},{10,... | collective-permute-start | bytes 393224 | tf_op jit(solution)/shard_map/ppermute | solution.py:299
  126.6 77.1 %collective-permute-start.13 = (bf16[1,256,256]{2,1,0:T(8,128)(2,1)S(1)}, bf16[1,256,256]{2,1,0:T(8,128)(2,1)}, u32[]{:S(2)}, u32[]{:S(2)}) collective-permute-start(bf16[1,256,256]{2,1,0:T(8,128)(2,1)S(1)} %collective-permute-done.9.refs_7_), channel_id=1, source_target_pairs={{0,2},{1,7},{2,4},{3,1},{4,6},{5,3},{6,0},{7,5},{8,10},{9,15},{10,... | collective-permute-start | bytes 393224 | tf_op jit(solution)/shard_map/ppermute | solution.py:299
  (44 other events, 2352.9 us)

commit v2 on v1

--- a/solution.py
+++ b/solution.py
@@ -35,6 +35,10 @@
 
 def iota(shape, dim):
     return lax.broadcasted_iota(jnp.int32, shape, dim)
+
+
+def cost(us):
+    return pl.CostEstimate(flops=int(us * 900e6), transcendentals=0, bytes_accessed=int(us * 1e6))
 
 
 def time_kernel(scale, pieces, chunks, gain_ref, wq_ref, wk_ref, wv_ref, wo_ref, *refs):
@@ -94,13 +98,14 @@
         out_shape=[jax.ShapeDtypeStruct((step, tokens, width), BF16)] * count,
         scratch_shapes=[pltpu.VMEM((frames, tile, width), F32)] * 4,
         compiler_params=pltpu.CompilerParams(vmem_limit_bytes=48 << 20),
+        cost_estimate=cost(18),
         name="time_attention",
     )(gain, wq, wk, wv, wo, *pieces)
 
 
-def space_kernel(scale, pieces, has_prev, ids, pos, gain_ref, wq_ref, wk_ref, wv_ref, wo_ref, cos_ref, sin_ref, *refs):
-    x_refs = refs[: 3 * pieces]
-    refs = refs[3 * pieces + (1 if has_prev else 0) :]
+def space_kernel(scale, pieces, has_prev, ids, pos, wq_ref, wk_ref, wv_ref, wo_ref, cos_ref, sin_ref, *refs):
+    x_refs, n_refs = refs[:pieces], refs[pieces : pieces + 3]
+    refs = refs[pieces + 3 + (1 if has_prev else 0) :]
     o_ref, wq_s, wk_s, q_s, k_s, v_s, x_s, kg, vg, flag = refs
     frame, block = pl.program_id(0), pl.program_id(1)
     piece_rows, width = x_refs[0].shape[1:]
@@ -135,11 +140,19 @@
         k_top, q_top = None, None
         for side in range(3):
             for i in range(pieces):
-                x_raw = x_refs[side * pieces + i][0]
-                normed = rms_rows(x_raw.astype(F32), gain_ref[...])
+                low = i * piece_rows
+                rows = slice(low, low + piece_rows)
+                normed = n_refs[side][0, rows, :]
                 at = pl.ds(pl.multiple_of(pos[i], piece_rows), piece_rows)
                 c, s = cos_ref[at, :], sin_ref[at, :]
-                low = (side * pieces + i) * piece_rows
+                if side == 0:
+                    u, w = turn(mm(normed, wq_s[...]) * scale, c, s)
+                    q_s[rows, :half] = u.astype(BF16)
+                    q_s[rows, half:] = w.astype(BF16)
+                    top = head_squares(u, w)
+                    q_top = top if q_top is None else jnp.maximum(q_top, top)
+                    x_s[rows, :] = x_refs[i][0]
+                low += side * pieces * piece_rows
                 rows = slice(low, low + piece_rows)
                 u, w = turn(mm(normed, wk_s[...]), c, s)
                 k_s[rows, :half] = u.astype(BF16)
@@ -147,13 +160,6 @@
                 top = head_squares(u, w)
                 k_top = top if k_top is None else jnp.maximum(k_top, top)
                 v_s[rows, :] = mm(normed, wv_ref[...]).astype(BF16)
-                if side == 0:
-                    u, w = turn(mm(normed, wq_s[...]) * scale, c, s)
-                    q_s[rows, :half] = u.astype(BF16)
-                    q_s[rows, half:] = w.astype(BF16)
-                    top = head_squares(u, w)
-                    q_top = top if q_top is None else jnp.maximum(q_top, top)
-                    x_s[rows, :] = x_raw
         flag[0] = jnp.max(k_top * q_top)
 
     for m in range(NEIGHBOUR_COUNT):
@@ -197,18 +203,36 @@
         attend(2, True)
 
 
-def space_stage(sides, ids, pos, gain, wq, wk, wv, wo, cos, sin, prev, chunk, chunks):
-    pieces = len(sides[0])
-    step, piece_rows, width = sides[0][0].shape
+def norm_kernel(pieces, gain_ref, *refs):
+    rows = refs[0].shape[1]
+    for i in range(pieces):
+        refs[pieces][:, i * rows : (i + 1) * rows, :] = rms_rows(refs[i][...].astype(F32), gain_ref[...])
+
+
+def norm_stage(own, gain):
+    step, rows, width = own[0].shape
+    shape = (step, rows * len(own), width)
+    return pl.pallas_call(
+        functools.partial(norm_kernel, len(own)),
+        out_shape=jax.ShapeDtypeStruct(shape, BF16),
+        compiler_params=pltpu.CompilerParams(vmem_limit_bytes=48 << 20),
+        cost_estimate=cost(2),
+        name="norm_join",
+    )(gain, *own)
+
+
+def space_stage(own, normed, ids, pos, wq, wk, wv, wo, cos, sin, prev, chunk, chunks):
+    pieces = len(own)
+    step, piece_rows, width = own[0].shape
     tokens = pieces * piece_rows
     blocks = tokens // BLOCK
     scale = LOG2E / float(np.sqrt(width // HEADS))
     full = pl.BlockSpec((width, width), lambda f, b, *_: (0, 0))
     table = pl.BlockSpec(cos.shape, lambda f, b, *_: (0, 0))
     piece = pl.BlockSpec((1, piece_rows, width), lambda f, b, *_: (f, 0, 0))
-    in_specs = [pl.BlockSpec((1, width), lambda f, b, *_: (0, 0))] + [full] * 4 + [table] * 2
-    in_specs += [piece] * (3 * pieces)
-    args = [gain, wq, wk, wv, wo, cos, sin] + [p for side in sides for p in side]
+    whole = pl.BlockSpec((1, tokens, width), lambda f, b, *_: (f, 0, 0))
+    in_specs = [full] * 4 + [table] * 2 + [piece] * pieces + [whole] * 3
+    args = [wq, wk, wv, wo, cos, sin, *own, *normed]
     aliases = {}
     if prev is not None:
         in_specs.append(pl.BlockSpec(memory_space=pl.ANY))
@@ -238,6 +262,7 @@
         out_shape=jax.ShapeDtypeStruct((step * chunks, tokens, width), BF16),
         input_output_aliases=aliases,
         compiler_params=pltpu.CompilerParams(vmem_limit_bytes=56 << 20),
+        cost_estimate=cost(20 * step),
         name="space_attention",
     )(ids, pos, *args)
 
@@ -288,16 +313,16 @@
     onward = [(i, (i + 2) % tile_count if i % 2 == 0 else (i - 2) % tile_count) for i in range(tile_count)]
     split = rows % BLOCK == 0
     places = me ^ jnp.arange(frame_count, dtype=jnp.int32)
-    sides = []
+    owns, nears = [], []
     for j in range(chunks):
         own = [outs[k * chunks + j] for k in range(frame_count)]
         own = [p if k == 0 else swap(p, k) for k, p in enumerate(own)]
         if not split:
             stacked = jnp.stack(own, axis=1)[:, places]
             own = [stacked.reshape(-1, tokens_here, width)]
-        near = [lax.ppermute(p, "tile", pairs) for p in own]
-        far = [lax.ppermute(p, "tile", onward) for p in near]
-        sides.append((own, near, far))
+        owns.append(own)
+        normed = norm_stage(own, gain_space.reshape(1, width))
+        nears.append((normed, lax.ppermute(normed, "tile", pairs)))
 
     blocks = tokens_here // BLOCK
     total = blocks * tile_count
@@ -321,11 +346,21 @@
     ).reshape(-1)
     cos, sin = rotary_tables(tokens_here, width)
     result = None
+    far = lax.ppermute(nears[0][1], "tile", onward)
     for j in range(chunks):
+        later = None
+        normed, near = nears[j]
+        if j + 1 < chunks:
+            if result is None:
+                normed, nears[j + 1] = lax.optimization_barrier((normed, nears[j + 1]))
+            else:
+                normed, nears[j + 1], result = lax.optimization_barrier((normed, nears[j + 1], result))
+            later = lax.ppermute(nears[j + 1][1], "tile", onward)
         result = space_stage(
-            sides[j], ids, pos, gain_space.reshape(1, width), query_space, key_space, value_space,
+            owns[j], (normed, near, far), ids, pos, query_space, key_space, value_space,
             output_space, cos, sin, result, j, chunks,
         )
+        far = later
     return result
 
 

time: 231 us -> 192 us (0.83); the launches traced: 229 us -> 192 us
  starting transfers between devices: 53.8 us -> 26.6 us
  waiting for transfers between devices: 51.3 us -> 37.6 us
  local copies, waits for them, and re-layouts: 3.79 us -> 8 us
    ppermute x32 -> x8, starting transfers between devices: 42.6 us -> 13.8 us  [the longest x4 9.85 us: body(): nears.append((normed, lax.ppermute(normed, 'tile', pairs)))]
    ppermute x32 -> x8, waiting for transfers between devices: 20.6 us -> 1.23 us  [the longest x4 1.22 us: body(): nears.append((normed, lax.ppermute(normed, 'tile', pairs)))]
    ppermute x15, waiting for transfers between devices: 30.7 us -> 36.4 us  [swap(): lax.ppermute(value, 'frame', [(i, i ^ k) for i in range(frame_count)])]
    unnamed x90 -> x72, local copies, waits for them, and re-layouts: 1.42 us -> 4.6 us
  transfers between devices with their start and end apart: 47 -> 23, of which waited for: 20 -> 9; matrix products, arithmetic and copies ran while one was open for 1% -> 1% of each run, Pallas kernels for 33% -> 39%
where the time goes in v2:
time: 192 us
  Pallas kernels  119 us (62%)
  waiting for transfers between devices  37.6 us (20%)
  starting transfers between devices  26.6 us (14%)
  local copies, waits for them, and re-layouts  8 us (4%)
    pallas_call x4, Pallas kernels, space_stage(): pl.pallas_call(functools.partial(space_kernel, scale, pieces, prev is not...  99.2 us
    ppermute x15, waiting for transfers between devices, swap(): lax.ppermute(value, 'frame', [(i, i ^ k) for i in range(frame_count)])  36.4 us
    pallas_call x1, Pallas kernels, time_stage(): pl.pallas_call(functools.partial(time_kernel, scale, len(pieces), chunks)...  18.8 us
    ppermute x15, starting transfers between devices, swap(): lax.ppermute(value, 'frame', [(i, i ^ k) for i in range(frame_count)])  12.8 us
    ppermute x4, starting transfers between devices, body(): nears.append((normed, lax.ppermute(normed, 'tile', pairs)))  9.85 us
    unnamed x72, local copies, waits for them, and re-layouts  4.6 us
  transfers between devices with their start and end apart: 23, of which 9 were waited for; matrix products, arithmetic and copies ran while one was open for 1% of the time, Pallas kernels for 39%

profile of v2, /device:TPU:0, one launch (start us, length us, event | category | flops | bytes accessed | tf_op | source)
XLA Modules:
  0.0 192.2 jit_solution(15268152176350454465)
XLA Ops:
  0.0 2.7 %constant_dynamic-slice_fusion = (bf16[4,256,256]{2,1,0:T(8,128)(2,1)S(1)}, bf16[4,256,256]{2,1,0:T(8,128)(2,1)}, bf16[4,256,256]{2,1,0:T(8,128)(2,1)S(1)}, bf16[4,256,256]{2,1,0:T(8,128)(2,1)}) fusion(bf16[4,1024,256]{2,1,0:T(8,128)(2,1)} %param.14, s32[]{:T(128)S(6)} %select_n.100, s32[]{:T(128)S(6)} %select_n.98, s32[]{:T(128)S(6)} %select_n.97, ...), kind=kLoop, calls=%fused_computation.48 | loop fusion | bytes 4194320 | tf_op jit(solution)/shard_map/dynamic_slice | solution.py:306
  2.8 0.5 collective-permute-start
  3.2 2.5 %collective-permute-start.1 = (bf16[4,256,256]{2,1,0:T(8,128)(2,1)}, bf16[4,256,256]{2,1,0:T(8,128)(2,1)S(1)}, u32[]{:S(2)}, u32[]{:S(2)}) collective-permute-start(bf16[4,256,256]{2,1,0:T(8,128)(2,1)} %get-tuple-element.62), channel_id=1, source_target_pairs={{0,16},{8,24},{16,0},{24,8},{1,17},{9,25},{17,1},{25,9},{2,18},{10... | collective-permute-start | bytes 1572872 | tf_op jit(solution)/shard_map/ppermute | solution.py:302
  5.7 0.1 collective-permute-start.2
  5.9 12.8 %collective-permute-done.1.refs_2_ = bf16[4,256,256]{2,1,0:T(8,128)(2,1)S(1)} collective-permute-done((bf16[4,256,256]{2,1,0:T(8,128)(2,1)}, bf16[4,256,256]{2,1,0:T(8,128)(2,1)S(1)}, u32[]{:S(2)}, u32[]{:S(2)}) %collective-permute-start.1) | collective-permute-done | bytes 524320 | tf_op jit(solution)/shard_map/ppermute | solution.py:302
  18.7 10.9 %collective-permute-done.2.refs_3_ = bf16[4,256,256]{2,1,0:T(8,128)(2,1)S(1)} collective-permute-done((bf16[4,256,256]{2,1,0:T(8,128)(2,1)S(1)}, bf16[4,256,256]{2,1,0:T(8,128)(2,1)S(1)}, u32[]{:S(2)}, u32[]{:S(2)}) %collective-permute-start.2) | collective-permute-done | bytes 524320 | tf_op jit(solution)/shard_map/ppermute | solution.py:302
  29.6 18.8 %time_attention.1 = (bf16[1,256,256]{2,1,0:T(8,128)(2,1)S(1)}, bf16[1,256,256]{2,1,0:T(8,128)(2,1)S(1)}, bf16[1,256,256]{2,1,0:T(8,128)(2,1)S(1)}, bf16[1,256,25...) custom-call(f32[1,256]{1,0:T(1,128)S(1)} %bitcast.2, ...), custom_call_target="tpu_custom_call" | custom-call | flops 16199999488 | bytes 18000000 | tf_op jit(solution)/shard_map/time_attention/pallas_call | solution.py:91
  48.4 0.2 collective-permute-start.6
  48.6 1.6 collective-permute-start.7
  50.3 0.1 collective-permute-start.8
  50.5 4.4 %collective-permute-done.7.refs_2_ = bf16[1,256,256]{2,1,0:T(8,128)(2,1)S(1)} collective-permute-done((bf16[1,256,256]{2,1,0:T(8,128)(2,1)S(1)}, bf16[1,256,256]{2,1,0:T(8,128)(2,1)S(1)}, u32[]{:S(2)}, u32[]{:S(2)}) %collective-permute-start.7) | collective-permute-done | bytes 131104 | tf_op jit(solution)/shard_map/ppermute | solution.py:302
  54.9 1.9 collective-permute-done.8.refs_3_
  56.8 0.2 norm_join.4.refs_4_
  57.1 0.4 copy-done.10
  57.5 1.4 collective-permute-start.17
  58.9 1.5 collective-permute-start.10
  60.4 0.6 collective-permute-start.9
  61.2 4.0 %collective-permute-done.10.refs_2_ = bf16[1,256,256]{2,1,0:T(8,128)(2,1)S(1)} collective-permute-done((bf16[1,256,256]{2,1,0:T(8,128)(2,1)S(1)}, bf16[1,256,256]{2,1,0:T(8,128)(2,1)S(1)}, u32[]{:S(2)}, u32[]{:S(2)}) %collective-permute-start.10) | collective-permute-done | bytes 131104 | tf_op jit(solution)/shard_map/ppermute | solution.py:302
  65.2 1.5 collective-permute-start.14
  66.7 0.3 collective-permute-done.11.refs_3_
  67.0 2.2 %collective-permute-start.15 = (bf16[1,256,256]{2,1,0:T(8,128)(2,1)S(1)}, bf16[1,256,256]{2,1,0:T(8,128)(2,1)S(1)}, u32[]{:S(2)}, u32[]{:S(2)}) collective-permute-start(bf16[1,256,256]{2,1,0:T(8,128)(2,1)S(1)} %get-tuple-element.48), channel_id=1, source_target_pairs={{0,24},{8,16},{16,8},{24,0},{1,25},{9,17},{17,9},{25,1},{2,26},{10... | collective-permute-start | bytes 393224 | tf_op jit(solution)/shard_map/ppermute | solution.py:302
  69.2 0.2 norm_join.5.refs_4_
  69.5 0.4 copy-done.15
  69.9 0.5 collective-permute-start.12
  70.4 1.2 collective-permute-done.17.refs_5_
  71.6 1.6 collective-permute-start.18
  73.3 0.7 reshape.71.ids
  74.0 0.5 xor_multiply_fusion.pos
  74.5 1.6 collective-permute-start.4
  76.1 0.3 collective-permute-start.5
  76.4 0.2 norm_join.6.refs_4_
  76.7 0.1 copy-done.16
  76.8 4.0 %collective-permute-start.16 = (bf16[1,1024,256]{2,1,0:T(8,128)(2,1)S(1)}, bf16[1,1024,256]{2,1,0:T(8,128)(2,1)S(1)}, u32[]{:S(2)}, u32[]{:S(2)}) collective-permute-start(bf16[1,1024,256]{2,1,0:T(8,128)(2,1)S(1)} %norm_join.6.refs_4_), channel_id=1, source_target_pairs={{0,1},{1,0},{2,3},{3,2},{4,5},{5,4},{6,7},{7,6},{8,9},{9,8},{10,11... | collective-permute-start | bytes 1572872 | tf_op jit(solution)/shard_map/ppermute | solution.py:325
  80.8 0.1 collective-permute-done.4.refs_2_
  80.9 1.9 collective-permute-done.5.refs_3_
  82.8 0.2 norm_join.7.refs_4_
  83.1 0.4 copy-done.19
  83.5 3.9 %collective-permute-start.19 = (bf16[1,1024,256]{2,1,0:T(8,128)(2,1)S(1)}, bf16[1,1024,256]{2,1,0:T(8,128)(2,1)S(1)}, u32[]{:S(2)}, u32[]{:S(2)}) collective-permute-start(bf16[1,1024,256]{2,1,0:T(8,128)(2,1)S(1)} %norm_join.7.refs_4_), channel_id=1, source_target_pairs={{0,1},{1,0},{2,3},{3,2},{4,5},{5,4},{6,7},{7,6},{8,9},{9,8},{10,11... | collective-permute-start | bytes 1572872 | tf_op jit(solution)/shard_map/ppermute | solution.py:325
  87.4 0.8 copy-done.30
  88.3 24.8 %space_attention.4.refs_7_ = bf16[4,1024,256]{2,1,0:T(8,128)(2,1)} custom-call(s32[88]{0:T(128)} %reshape.71.ids, s32[4]{0:T(128)} %xor_multiply_fusion.pos, bf16[256,256]{1,0:T(8,128)(2,1)} %wq_ref.9, bf16[256,256]{1,0:T(8,128)(2,1)} %wk_ref.9, bf16[256,256]{1,0:T(8,128)(2,1)} %wv_ref.9, bf16[256,256]{1,0:T(8,128)(2,1)} %wo_ref.9, ...), custom_call_target="tpu_custom_call" | custom-call | flops 17999998976 | bytes 20000000 | tf_op jit(solution)/shard_map/space_attention/pallas_call | solution.py:259
  113.1 0.7 collective-permute-start.22
  113.8 0.8 copy-done.34
  114.6 24.8 %space_attention.5.refs_7_ = bf16[4,1024,256]{2,1,0:T(8,128)(2,1)} custom-call(s32[88]{0:T(128)} %reshape.71.ids, s32[4]{0:T(128)} %xor_multiply_fusion.pos, bf16[256,256]{1,0:T(8,128)(2,1)} %wq_ref.9, bf16[256,256]{1,0:T(8,128)(2,1)} %wk_ref.9, bf16[256,256]{1,0:T(8,128)(2,1)} %wv_ref.9, bf16[256,256]{1,0:T(8,128)(2,1)} %wo_ref.9, ...), custom_call_target="tpu_custom_call", output_to_operand_aliasing={{}: (15, {})} | custom-call | flops 17999998976 | bytes 20000000 | tf_op jit(solution)/shard_map/space_attention/pallas_call | solution.py:259
  139.4 1.6 collective-permute-start.21
  141.0 0.8 copy-done.33
  141.8 24.8 %space_attention.6.refs_7_ = bf16[4,1024,256]{2,1,0:T(8,128)(2,1)} custom-call(s32[88]{0:T(128)} %reshape.71.ids, s32[4]{0:T(128)} %xor_multiply_fusion.pos, bf16[256,256]{1,0:T(8,128)(2,1)} %wq_ref.9, bf16[256,256]{1,0:T(8,128)(2,1)} %wk_ref.9, bf16[256,256]{1,0:T(8,128)(2,1)} %wv_ref.9, bf16[256,256]{1,0:T(8,128)(2,1)} %wo_ref.9, ...), custom_call_target="tpu_custom_call", output_to_operand_aliasing={{}: (15, {})} | custom-call | flops 17999998976 | bytes 20000000 | tf_op jit(solution)/shard_map/space_attention/pallas_call | solution.py:259
  166.6 0.8 copy-done.35
  167.4 24.8 %space_attention.7 = bf16[4,1024,256]{2,1,0:T(8,128)(2,1)} custom-call(s32[88]{0:T(128)} %reshape.71.ids, s32[4]{0:T(128)} %xor_multiply_fusion.pos, bf16[256,256]{1,0:T(8,128)(2,1)} %wq_ref.9, bf16[256,256]{1,0:T(8,128)(2,1)} %wk_ref.9, bf16[256,256]{1,0:T(8,128)(2,1)} %wv_ref.9, bf16[256,256]{1,0:T(8,128)(2,1)} %wo_ref.9, ...), custom_call_target="tpu_custom_call", output_to_operand_aliasing={{}: (15, {})} | custom-call | flops 17999998976 | bytes 20000000 | tf_op jit(solution)/shard_map/space_attention/pallas_call | solution.py:259
  (88 shorter events, 0.5 us)
Async XLA Ops:
  0.0 29.6 %copy-start.4 = (bf16[256,256]{1,0:T(8,128)(2,1)S(1)}, bf16[256,256]{1,0:T(8,128)(2,1)}, u32[]{:S(2)}) copy-start(bf16[256,256]{1,0:T(8,128)(2,1)} %wq_ref.5) | copy-start | bytes 393220
  0.0 29.6 %copy-start.5 = (bf16[256,256]{1,0:T(8,128)(2,1)S(1)}, bf16[256,256]{1,0:T(8,128)(2,1)}, u32[]{:S(2)}) copy-start(bf16[256,256]{1,0:T(8,128)(2,1)} %wk_ref.5) | copy-start | bytes 393220
  0.0 29.6 %copy-start.6 = (bf16[256,256]{1,0:T(8,128)(2,1)S(1)}, bf16[256,256]{1,0:T(8,128)(2,1)}, u32[]{:S(2)}) copy-start(bf16[256,256]{1,0:T(8,128)(2,1)} %wv_ref.5) | copy-start | bytes 393220
  0.0 29.6 %copy-start.7 = (bf16[256,256]{1,0:T(8,128)(2,1)S(1)}, bf16[256,256]{1,0:T(8,128)(2,1)}, u32[]{:S(2)}) copy-start(bf16[256,256]{1,0:T(8,128)(2,1)} %wo_ref.5) | copy-start | bytes 393220
  0.0 29.6 %copy-start.20 = (f32[256]{0:T(256)S(1)}, f32[256]{0:T(256)}, u32[]{:S(2)}) copy-start(f32[256]{0:T(256)} %param.15) | copy-start | bytes 3076
  2.8 3.1 %collective-permute-start = (bf16[4,256,256]{2,1,0:T(8,128)(2,1)}, bf16[4,256,256]{2,1,0:T(8,128)(2,1)S(1)}, u32[]{:S(2)}, u32[]{:S(2)}) collective-permute-start(bf16[4,256,256]{2,1,0:T(8,128)(2,1)} %get-tuple-element.60), channel_id=1, source_target_pairs={{0,8},{8,0},{16,24},{24,16},{1,9},{9,1},{17,25},{25,17},{2,10},{10... | collective-permute-start | bytes 1572872 | tf_op jit(solution)/shard_map/ppermute | solution.py:302
  3.2 15.5 %collective-permute-start.1 = (bf16[4,256,256]{2,1,0:T(8,128)(2,1)}, bf16[4,256,256]{2,1,0:T(8,128)(2,1)S(1)}, u32[]{:S(2)}, u32[]{:S(2)}) collective-permute-start(bf16[4,256,256]{2,1,0:T(8,128)(2,1)} %get-tuple-element.62), channel_id=1, source_target_pairs={{0,16},{8,24},{16,0},{24,8},{1,17},{9,25},{17,1},{25,9},{2,18},{10... | collective-permute-start | bytes 1572872 | tf_op jit(solution)/shard_map/ppermute | solution.py:302
  5.7 23.9 %collective-permute-start.2 = (bf16[4,256,256]{2,1,0:T(8,128)(2,1)S(1)}, bf16[4,256,256]{2,1,0:T(8,128)(2,1)S(1)}, u32[]{:S(2)}, u32[]{:S(2)}) collective-permute-start(bf16[4,256,256]{2,1,0:T(8,128)(2,1)S(1)} %get-tuple-element.59), channel_id=1, source_target_pairs={{0,24},{8,16},{16,8},{24,0},{1,25},{9,17},{17,9},{25,1},{2,26},{10... | collective-permute-start | bytes 1572872 | tf_op jit(solution)/shard_map/ppermute | solution.py:302
  29.6 20.8 %copy-start.27 = (s32[8,9]{1,0:T(8,128)S(1)}, s32[8,9]{1,0:T(8,128)}, u32[]{:S(2)}) copy-start(s32[8,9]{1,0:T(8,128)} %param.25) | copy-start | bytes 868
  29.6 27.2 %copy-start.21 = (f32[256]{0:T(256)S(1)}, f32[256]{0:T(256)}, u32[]{:S(2)}) copy-start(f32[256]{0:T(256)} %param.20) | copy-start | bytes 3076
  48.4 8.6 %copy-start.23 = (bf16[1,256,256]{2,1,0:T(8,128)(2,1)}, bf16[1,256,256]{2,1,0:T(8,128)(2,1)S(1)}, u32[]{:S(2)}) copy-start(bf16[1,256,256]{2,1,0:T(8,128)(2,1)S(1)} %get-tuple-element.45.refs_0_) | copy-start | bytes 393220
  48.4 8.6 %copy-start.26 = (bf16[1,256,256]{2,1,0:T(8,128)(2,1)}, bf16[1,256,256]{2,1,0:T(8,128)(2,1)S(1)}, u32[]{:S(2)}) copy-start(bf16[1,256,256]{2,1,0:T(8,128)(2,1)S(1)} %get-tuple-element.36.refs_0_) | copy-start | bytes 393220
  48.4 20.8 %copy-start.25 = (bf16[1,256,256]{2,1,0:T(8,128)(2,1)}, bf16[1,256,256]{2,1,0:T(8,128)(2,1)S(1)}, u32[]{:S(2)}) copy-start(bf16[1,256,256]{2,1,0:T(8,128)(2,1)S(1)} %get-tuple-element.40.refs_0_) | copy-start | bytes 393220
  48.4 34.3 %copy-start.22 = (bf16[1,256,256]{2,1,0:T(8,128)(2,1)}, bf16[1,256,256]{2,1,0:T(8,128)(2,1)S(1)}, u32[]{:S(2)}) copy-start(bf16[1,256,256]{2,1,0:T(8,128)(2,1)S(1)} %get-tuple-element.32.refs_0_) | copy-start | bytes 393220
  48.4 2.0 %collective-permute-start.6 = (bf16[1,256,256]{2,1,0:T(8,128)(2,1)S(1)}, bf16[1,256,256]{2,1,0:T(8,128)(2,1)S(1)}, u32[]{:S(2)}, u32[]{:S(2)}) collective-permute-start(bf16[1,256,256]{2,1,0:T(8,128)(2,1)S(1)} %get-tuple-element.37), channel_id=1, source_target_pairs={{0,8},{8,0},{16,24},{24,16},{1,9},{9,1},{17,25},{25,17},{2,10},{10... | collective-permute-start | bytes 393224 | tf_op jit(solution)/shard_map/ppermute | solution.py:302
  48.6 6.3 %collective-permute-start.7 = (bf16[1,256,256]{2,1,0:T(8,128)(2,1)S(1)}, bf16[1,256,256]{2,1,0:T(8,128)(2,1)S(1)}, u32[]{:S(2)}, u32[]{:S(2)}) collective-permute-start(bf16[1,256,256]{2,1,0:T(8,128)(2,1)S(1)} %get-tuple-element.38), channel_id=1, source_target_pairs={{0,16},{8,24},{16,0},{24,8},{1,17},{9,25},{17,1},{25,9},{2,18},{10... | collective-permute-start | bytes 393224 | tf_op jit(solution)/shard_map/ppermute | solution.py:302
  50.3 6.5 %collective-permute-start.8 = (bf16[1,256,256]{2,1,0:T(8,128)(2,1)S(1)}, bf16[1,256,256]{2,1,0:T(8,128)(2,1)S(1)}, u32[]{:S(2)}, u32[]{:S(2)}) collective-permute-start(bf16[1,256,256]{2,1,0:T(8,128)(2,1)S(1)} %get-tuple-element.39), channel_id=1, source_target_pairs={{0,24},{8,16},{16,8},{24,0},{1,25},{9,17},{17,9},{25,1},{2,26},{10... | collective-permute-start | bytes 393224 | tf_op jit(solution)/shard_map/ppermute | solution.py:302
  50.5 6.6 %copy-start.8 = (bf16[1,256,256]{2,1,0:T(8,128)(2,1)}, bf16[1,256,256]{2,1,0:T(8,128)(2,1)S(1)}, u32[]{:S(2)}) copy-start(bf16[1,256,256]{2,1,0:T(8,128)(2,1)S(1)} %collective-permute-done.6.refs_1_) | copy-start | bytes 393220
  57.5 12.0 %copy-start = (bf16[1,1024,256]{2,1,0:T(8,128)(2,1)}, bf16[1,1024,256]{2,1,0:T(8,128)(2,1)S(1)}, u32[]{:S(2)}) copy-start(bf16[1,1024,256]{2,1,0:T(8,128)(2,1)S(1)} %norm_join.4.refs_4_) | copy-start | bytes 1572868
  57.5 14.2 %collective-permute-start.17 = (bf16[1,1024,256]{2,1,0:T(8,128)(2,1)S(1)}, bf16[1,1024,256]{2,1,0:T(8,128)(2,1)S(1)}, u32[]{:S(2)}, u32[]{:S(2)}) collective-permute-start(bf16[1,1024,256]{2,1,0:T(8,128)(2,1)S(1)} %norm_join.4.refs_4_), channel_id=1, source_target_pairs={{0,1},{1,0},{2,3},{3,2},{4,5},{5,4},{6,7},{7,6},{8,9},{9,8},{10,11... | collective-permute-start | bytes 1572872 | tf_op jit(solution)/shard_map/ppermute | solution.py:325
  58.9 6.3 %collective-permute-start.10 = (bf16[1,256,256]{2,1,0:T(8,128)(2,1)S(1)}, bf16[1,256,256]{2,1,0:T(8,128)(2,1)S(1)}, u32[]{:S(2)}, u32[]{:S(2)}) collective-permute-start(bf16[1,256,256]{2,1,0:T(8,128)(2,1)S(1)} %get-tuple-element.42), channel_id=1, source_target_pairs={{0,16},{8,24},{16,0},{24,8},{1,17},{9,25},{17,1},{25,9},{2,18},{10... | collective-permute-start | bytes 393224 | tf_op jit(solution)/shard_map/ppermute | solution.py:302
  60.3 6.7 %collective-permute-start.11 = (bf16[1,256,256]{2,1,0:T(8,128)(2,1)S(1)}, bf16[1,256,256]{2,1,0:T(8,128)(2,1)S(1)}, u32[]{:S(2)}, u32[]{:S(2)}) collective-permute-start(bf16[1,256,256]{2,1,0:T(8,128)(2,1)S(1)} %get-tuple-element.43), channel_id=1, source_target_pairs={{0,24},{8,16},{16,8},{24,0},{1,25},{9,17},{17,9},{25,1},{2,26},{10... | collective-permute-start | bytes 393224 | tf_op jit(solution)/shard_map/ppermute | solution.py:302
  60.4 8.8 %collective-permute-start.9 = (bf16[1,256,256]{2,1,0:T(8,128)(2,1)S(1)}, bf16[1,256,256]{2,1,0:T(8,128)(2,1)S(1)}, u32[]{:S(2)}, u32[]{:S(2)}) collective-permute-start(bf16[1,256,256]{2,1,0:T(8,128)(2,1)S(1)} %get-tuple-element.41), channel_id=1, source_target_pairs={{0,8},{8,0},{16,24},{24,16},{1,9},{9,1},{17,25},{25,17},{2,10},{10... | collective-permute-start | bytes 393224 | tf_op jit(solution)/shard_map/ppermute | solution.py:302
  61.1 13.4 %collective-permute-start.13 = (bf16[1,256,256]{2,1,0:T(8,128)(2,1)S(1)}, bf16[1,256,256]{2,1,0:T(8,128)(2,1)S(1)}, u32[]{:S(2)}, u32[]{:S(2)}) collective-permute-start(bf16[1,256,256]{2,1,0:T(8,128)(2,1)S(1)} %get-tuple-element.46), channel_id=1, source_target_pairs={{0,8},{8,0},{16,24},{24,16},{1,9},{9,1},{17,25},{25,17},{2,10},{10... | collective-permute-start | bytes 393224 | tf_op jit(solution)/shard_map/ppermute | solution.py:302
  65.2 4.3 %copy-start.12 = (bf16[1,256,256]{2,1,0:T(8,128)(2,1)}, bf16[1,256,256]{2,1,0:T(8,128)(2,1)S(1)}, u32[]{:S(2)}) copy-start(bf16[1,256,256]{2,1,0:T(8,128)(2,1)S(1)} %collective-permute-done.10.refs_2_) | copy-start | bytes 393220
  65.2 9.3 %collective-permute-start.14 = (bf16[1,256,256]{2,1,0:T(8,128)(2,1)S(1)}, bf16[1,256,256]{2,1,0:T(8,128)(2,1)S(1)}, u32[]{:S(2)}, u32[]{:S(2)}) collective-permute-start(bf16[1,256,256]{2,1,0:T(8,128)(2,1)S(1)} %get-tuple-element.47), channel_id=1, source_target_pairs={{0,16},{8,24},{16,0},{24,8},{1,17},{9,25},{17,1},{25,9},{2,18},{10... | collective-permute-start | bytes 393224 | tf_op jit(solution)/shard_map/ppermute | solution.py:302
  67.0 2.5 %copy-start.13 = (bf16[1,256,256]{2,1,0:T(8,128)(2,1)}, bf16[1,256,256]{2,1,0:T(8,128)(2,1)S(1)}, u32[]{:S(2)}) copy-start(bf16[1,256,256]{2,1,0:T(8,128)(2,1)S(1)} %collective-permute-done.11.refs_3_) | copy-start | bytes 393220
  67.0 9.1 %collective-permute-start.15 = (bf16[1,256,256]{2,1,0:T(8,128)(2,1)S(1)}, bf16[1,256,256]{2,1,0:T(8,128)(2,1)S(1)}, u32[]{:S(2)}, u32[]{:S(2)}) collective-permute-start(bf16[1,256,256]{2,1,0:T(8,128)(2,1)S(1)} %get-tuple-element.48), channel_id=1, source_target_pairs={{0,24},{8,16},{16,8},{24,0},{1,25},{9,17},{17,9},{25,1},{2,26},{10... | collective-permute-start | bytes 393224 | tf_op jit(solution)/shard_map/ppermute | solution.py:302
  69.2 7.2 %copy-start.24 = (bf16[1,256,256]{2,1,0:T(8,128)(2,1)S(1)}, bf16[1,256,256]{2,1,0:T(8,128)(2,1)}, u32[]{:S(2)}) copy-start(bf16[1,256,256]{2,1,0:T(8,128)(2,1)} %copy-done.23) | copy-start | bytes 393220
  69.9 6.7 %copy-start.1 = (bf16[1,1024,256]{2,1,0:T(8,128)(2,1)}, bf16[1,1024,256]{2,1,0:T(8,128)(2,1)S(1)}, u32[]{:S(2)}) copy-start(bf16[1,1024,256]{2,1,0:T(8,128)(2,1)S(1)} %norm_join.5.refs_4_) | copy-start | bytes 1572868
  69.9 17.5 %collective-permute-start.12 = (bf16[1,1024,256]{2,1,0:T(8,128)(2,1)S(1)}, bf16[1,1024,256]{2,1,0:T(8,128)(2,1)S(1)}, u32[]{:S(2)}, u32[]{:S(2)}) collective-permute-start(bf16[1,1024,256]{2,1,0:T(8,128)(2,1)S(1)} %norm_join.5.refs_4_), channel_id=1, source_target_pairs={{0,1},{1,0},{2,3},{3,2},{4,5},{5,4},{6,7},{7,6},{8,9},{9,8},{10,11... | collective-permute-start | bytes 1572872 | tf_op jit(solution)/shard_map/ppermute | solution.py:325
  71.6 5.0 %copy-start.28 = (bf16[1,1024,256]{2,1,0:T(8,128)(2,1)}, bf16[1,1024,256]{2,1,0:T(8,128)(2,1)S(1)}, u32[]{:S(2)}) copy-start(bf16[1,1024,256]{2,1,0:T(8,128)(2,1)S(1)} %collective-permute-done.17.refs_5_) | copy-start | bytes 1572868
  71.6 15.8 %collective-permute-start.18 = (bf16[1,1024,256]{2,1,0:T(8,128)(2,1)S(1)}, bf16[1,1024,256]{2,1,0:T(8,128)(2,1)S(1)}, u32[]{:S(2)}, u32[]{:S(2)}) collective-permute-start(bf16[1,1024,256]{2,1,0:T(8,128)(2,1)S(1)} %collective-permute-done.17.refs_5_), channel_id=1, source_target_pairs={{0,2},{1,7},{2,4},{3,1},{4,6},{5,3},{6,0},{7,5},{8,10},{9,15},{10,... | collective-permute-start | bytes 1572872 | tf_op jit(solution)/shard_map/ppermute | solution.py:349
  74.5 2.1 %copy-start.11 = (bf16[1,256,256]{2,1,0:T(8,128)(2,1)}, bf16[1,256,256]{2,1,0:T(8,128)(2,1)S(1)}, u32[]{:S(2)}) copy-start(bf16[1,256,256]{2,1,0:T(8,128)(2,1)S(1)} %collective-permute-done.13.refs_1_) | copy-start | bytes 393220
  74.5 2.3 %collective-permute-start.3 = (bf16[1,256,256]{2,1,0:T(8,128)(2,1)S(1)}, bf16[1,256,256]{2,1,0:T(8,128)(2,1)S(1)}, u32[]{:S(2)}, u32[]{:S(2)}) collective-permute-start(bf16[1,256,256]{2,1,0:T(8,128)(2,1)S(1)} %get-tuple-element.33), channel_id=1, source_target_pairs={{0,8},{8,0},{16,24},{24,16},{1,9},{9,1},{17,25},{25,17},{2,10},{10... | collective-permute-start | bytes 393224 | tf_op jit(solution)/shard_map/ppermute | solution.py:302
  74.5 6.4 %collective-permute-start.4 = (bf16[1,256,256]{2,1,0:T(8,128)(2,1)S(1)}, bf16[1,256,256]{2,1,0:T(8,128)(2,1)S(1)}, u32[]{:S(2)}, u32[]{:S(2)}) collective-permute-start(bf16[1,256,256]{2,1,0:T(8,128)(2,1)S(1)} %get-tuple-element.34), channel_id=1, source_target_pairs={{0,16},{8,24},{16,0},{24,8},{1,17},{9,25},{17,1},{25,9},{2,18},{10... | collective-permute-start | bytes 393224 | tf_op jit(solution)/shard_map/ppermute | solution.py:302
  76.1 6.7 %collective-permute-start.5 = (bf16[1,256,256]{2,1,0:T(8,128)(2,1)S(1)}, bf16[1,256,256]{2,1,0:T(8,128)(2,1)S(1)}, u32[]{:S(2)}, u32[]{:S(2)}) collective-permute-start(bf16[1,256,256]{2,1,0:T(8,128)(2,1)S(1)} %get-tuple-element.35), channel_id=1, source_target_pairs={{0,24},{8,16},{16,8},{24,0},{1,25},{9,17},{17,9},{25,1},{2,26},{10... | collective-permute-start | bytes 393224 | tf_op jit(solution)/shard_map/ppermute | solution.py:302
  76.8 6.3 %copy-start.2 = (bf16[1,1024,256]{2,1,0:T(8,128)(2,1)}, bf16[1,1024,256]{2,1,0:T(8,128)(2,1)S(1)}, u32[]{:S(2)}) copy-start(bf16[1,1024,256]{2,1,0:T(8,128)(2,1)S(1)} %norm_join.6.refs_4_) | copy-start | bytes 1572868
  76.8 6.3 %copy-start.17 = (bf16[1,256,256]{2,1,0:T(8,128)(2,1)}, bf16[1,256,256]{2,1,0:T(8,128)(2,1)S(1)}, u32[]{:S(2)}) copy-start(bf16[1,256,256]{2,1,0:T(8,128)(2,1)S(1)} %collective-permute-done.3.refs_1_) | copy-start | bytes 393220
  76.8 36.3 %collective-permute-start.16 = (bf16[1,1024,256]{2,1,0:T(8,128)(2,1)S(1)}, bf16[1,1024,256]{2,1,0:T(8,128)(2,1)S(1)}, u32[]{:S(2)}, u32[]{:S(2)}) collective-permute-start(bf16[1,1024,256]{2,1,0:T(8,128)(2,1)S(1)} %norm_join.6.refs_4_), channel_id=1, source_target_pairs={{0,1},{1,0},{2,3},{3,2},{4,5},{5,4},{6,7},{7,6},{8,9},{9,8},{10,11... | collective-permute-start | bytes 1572872 | tf_op jit(solution)/shard_map/ppermute | solution.py:325
  83.5 29.6 %copy-start.3 = (bf16[1,1024,256]{2,1,0:T(8,128)(2,1)}, bf16[1,1024,256]{2,1,0:T(8,128)(2,1)S(1)}, u32[]{:S(2)}) copy-start(bf16[1,1024,256]{2,1,0:T(8,128)(2,1)S(1)} %norm_join.7.refs_4_) | copy-start | bytes 1572868
  83.5 55.9 %collective-permute-start.19 = (bf16[1,1024,256]{2,1,0:T(8,128)(2,1)S(1)}, bf16[1,1024,256]{2,1,0:T(8,128)(2,1)S(1)}, u32[]{:S(2)}, u32[]{:S(2)}) collective-permute-start(bf16[1,1024,256]{2,1,0:T(8,128)(2,1)S(1)} %norm_join.7.refs_4_), channel_id=1, source_target_pairs={{0,1},{1,0},{2,3},{3,2},{4,5},{5,4},{6,7},{7,6},{8,9},{9,8},{10,11... | collective-permute-start | bytes 1572872 | tf_op jit(solution)/shard_map/ppermute | solution.py:325
  87.4 25.7 %copy-start.29 = (bf16[1,1024,256]{2,1,0:T(8,128)(2,1)}, bf16[1,1024,256]{2,1,0:T(8,128)(2,1)S(1)}, u32[]{:S(2)}) copy-start(bf16[1,1024,256]{2,1,0:T(8,128)(2,1)S(1)} %collective-permute-done.12.refs_5_) | copy-start | bytes 1572868
  87.4 26.4 %collective-permute-start.20 = (bf16[1,1024,256]{2,1,0:T(8,128)(2,1)S(1)}, bf16[1,1024,256]{2,1,0:T(8,128)(2,1)S(1)}, u32[]{:S(2)}, u32[]{:S(2)}) collective-permute-start(bf16[1,1024,256]{2,1,0:T(8,128)(2,1)S(1)} %collective-permute-done.12.refs_5_), channel_id=1, source_target_pairs={{0,2},{1,7},{2,4},{3,1},{4,6},{5,3},{6,0},{7,5},{8,10},{9,15},{10,... | collective-permute-start | bytes 1572872 | tf_op jit(solution)/shard_map/ppermute | solution.py:358
  113.1 26.3 %copy-start.32 = (bf16[1,1024,256]{2,1,0:T(8,128)(2,1)}, bf16[1,1024,256]{2,1,0:T(8,128)(2,1)S(1)}, u32[]{:S(2)}) copy-start(bf16[1,1024,256]{2,1,0:T(8,128)(2,1)S(1)} %collective-permute-done.16.refs_5_) | copy-start | bytes 1572868
  113.1 27.9 %collective-permute-start.22 = (bf16[1,1024,256]{2,1,0:T(8,128)(2,1)S(1)}, bf16[1,1024,256]{2,1,0:T(8,128)(2,1)S(1)}, u32[]{:S(2)}, u32[]{:S(2)}) collective-permute-start(bf16[1,1024,256]{2,1,0:T(8,128)(2,1)S(1)} %collective-permute-done.16.refs_5_), channel_id=1, source_target_pairs={{0,2},{1,7},{2,4},{3,1},{4,6},{5,3},{6,0},{7,5},{8,10},{9,15},{10,... | collective-permute-start | bytes 1572872 | tf_op jit(solution)/shard_map/ppermute | solution.py:358
  139.4 27.2 %copy-start.31 = (bf16[1,1024,256]{2,1,0:T(8,128)(2,1)}, bf16[1,1024,256]{2,1,0:T(8,128)(2,1)S(1)}, u32[]{:S(2)}) copy-start(bf16[1,1024,256]{2,1,0:T(8,128)(2,1)S(1)} %collective-permute-done.19.refs_5_) | copy-start | bytes 1572868
  139.4 27.2 %collective-permute-start.21 = (bf16[1,1024,256]{2,1,0:T(8,128)(2,1)S(1)}, bf16[1,1024,256]{2,1,0:T(8,128)(2,1)S(1)}, u32[]{:S(2)}, u32[]{:S(2)}) collective-permute-start(bf16[1,1024,256]{2,1,0:T(8,128)(2,1)S(1)} %collective-permute-done.19.refs_5_), channel_id=1, source_target_pairs={{0,2},{1,7},{2,4},{3,1},{4,6},{5,3},{6,0},{7,5},{8,10},{9,15},{10,... | collective-permute-start | bytes 1572872 | tf_op jit(solution)/shard_map/ppermute | solution.py:358
  (11 other events, 12.3 us)
